TPU v7x, 32 devices: a whole 2x2x4 slice. The times are simulated.
32 devices in a mesh: section: 4 (over y, x), dp: 4 (over z), mp: 2 (over core).
Axes of the slice: x: 2, y: 2, z: 4, core: 2. Of those that a mesh axis runs over, the one named last changes fastest.
Arguments:
- inputs: bfloat16 [8, 256, 1536], P('dp', 'mp'), may hold values from -6 to 6
- cotangent: bfloat16 [8, 256, 1536], P('dp', 'mp'), may hold values from -6 to 6
- width_index: int32 [8], P('dp'), may hold values from 0 to 3, as said below
- qkv_weight: bfloat16 [3, 3072, 1536], P(None, 'section', 'mp'), may hold values from -0.15625 to 0.15625
- out_weight: bfloat16 [3072, 1536], P('section', 'mp'), may hold values from -1.75 to 1.75
- attn_gain: bfloat16 [3072], P('section'), may hold values from 0.5 to 1.5
- ffn_gain: bfloat16 [3072], P('section'), may hold values from 0.5 to 1.5
- up_weight: bfloat16 [3072, 6144], P('section', 'mp'), may hold values from -0.15625 to 0.15625
- down_weight: bfloat16 [3072, 6144], P('section', 'mp'), may hold values from -0.15625 to 0.15625
Outputs:
- layer_out: bfloat16 [4, 8, 256, 1536], P('section', 'dp', 'mp')
- input_grad: bfloat16 [4, 8, 256, 1536], P('section', 'dp', 'mp')
- qkv_grad: float32 [3, 3072, 1536], P(None, ('section', 'dp'), 'mp')
- out_weight_grad: float32 [3072, 1536], P(('section', 'dp'), 'mp')
- attn_gain_grad: float32 [3072], P(('section', 'dp', 'mp'))
- ffn_gain_grad: float32 [3072], P(('section', 'dp', 'mp'))
- up_grad: float32 [3072, 6144], P(('section', 'dp'), 'mp')
- down_grad: float32 [3072, 6144], P(('section', 'dp'), 'mp')
Inputs may be any that keep to these rules, and one draw needn't show every extreme that they name: `width_index`: in each aligned pair of sequences (2i and 2i+1) the two width indices add up to 3.
All inputs are finite; a program needn't handle non-finite values.
Results may differ from a plain program's by a relative error of at most 0.03.
Values may be sent and summed in bfloat16 or wider, within the bound.
A program may use at most 384 MiB of HBM per device.

v0:
```python
import jax
import jax.numpy as jnp
import numpy as np
from jax import lax
from jax.sharding import PartitionSpec as P
from jax.experimental import pallas as pl
from jax.experimental.pallas import tpu as pltpu

HEAD_DIM = 128
EPSILON = 1e-05
GELU_C = 0.7978845608028654
GELU_A = 0.044715
MESH = pl.DeviceIdType.MESH
SLOTS = 10
EARLY_STEPS = 2
DIRECT_ROWS = 144
F32 = jnp.float32
BF16 = jnp.bfloat16
VMEM_LIMIT = 62 * 2**20


def mm(a, b):
    return lax.dot_general(a, b, (((1,), (0,)), ((), ())), preferred_element_type=F32)


def mm_nt(a, b):
    return lax.dot_general(a, b, (((1,), (1,)), ((), ())), preferred_element_type=F32)


def mm_tn(a, b):
    return lax.dot_general(a, b, (((0,), (0,)), ((), ())), preferred_element_type=F32)


def to_row(column):
    rows = column.shape[0]
    return jnp.transpose(jnp.broadcast_to(column, (rows, 128)))[:8]


def from_row(row):
    return jnp.transpose(row)[:, :1]


def rotary(length, head_size):
    half_dim = head_size // 2
    frequency = np.float32(10000.0) ** (np.float32(-2.0 / head_size) * np.arange(half_dim, dtype=np.float32))
    angles = np.arange(length, dtype=np.float32)[:, None] * frequency[None, :].astype(np.float32)
    cosine, sine = np.cos(angles).astype(np.float32), np.sin(angles).astype(np.float32)
    return jnp.asarray(np.concatenate([cosine, cosine], axis=1)), jnp.asarray(np.concatenate([-sine, sine], axis=1))


def turned(values):
    return pltpu.roll(values, HEAD_DIM // 2, 1)


def remote(src, dst, send_sem, recv_sem, device):
    return pltpu.make_async_remote_copy(
        src_ref=src, dst_ref=dst, send_sem=send_sem, recv_sem=recv_sem,
        device_id=device, device_id_type=MESH,
    )


class Place:
    def __init__(self):
        section, dp, mp = (lax.axis_index(name) for name in ("section", "dp", "mp"))
        self.block, self.half, self.core = section // 2, section % 2, mp
        other_half = 1 - self.half
        other_block = 1 - self.block
        self.at = (section, dp, mp)
        self.core_peer = (section, dp, 1 - mp)
        self.pair = (self.block * 2 + other_half, dp, mp)
        self.across = (other_block * 2 + self.half, dp, mp)
        self.corner = (other_block * 2 + other_half, dp, mp)

    def plane(self, n):
        section, dp, mp = self.at
        return (section, lax.rem(dp + n, lax.axis_size("dp")), mp)

    def barrier(self):
        sem = pltpu.get_barrier_semaphore()
        peers = [self.core_peer, self.pair, self.across, self.corner]
        peers += [self.plane(n) for n in range(1, lax.axis_size("dp"))]
        for peer in peers:
            pl.semaphore_signal(sem, inc=1, device_id=peer, device_id_type=MESH)
        pl.semaphore_wait(sem, len(peers))


class Exchange:
    def __init__(self, place, piece, slots, sems):
        self.place, self.piece, self.slots = place, piece, slots
        self.send, self.recv, self.local = sems
        self.me, self.count = lax.axis_index("dp"), lax.axis_size("dp")

    def copy(self, n):
        target = lax.rem(self.me + n, self.count)
        return remote(self.piece(target), self.slots.at[self.me], self.send.at[n], self.recv.at[n], self.place.plane(n))

    def own(self):
        return pltpu.make_async_copy(self.piece(self.me), self.slots.at[self.me], self.local.at[0])

    def start(self):
        self.own().start()
        for n in range(1, self.count):
            self.copy(n).start()

    def finish(self):
        self.own().wait()
        for n in range(1, self.count):
            source = lax.rem(self.me + self.count - n, self.count)
            held = self.slots.at[source]
            remote(held, held, self.send.at[n], self.recv.at[n], self.place.plane(n)).wait_recv()
            self.copy(n).wait_send()


class PairLink:
    def __init__(self, place, relay, sems, targets):
        self.place, self.relay, self.targets = place, relay, targets
        self.send, self.recv, self.far_send, self.far_recv, self.relay_send, self.relay_recv = sems
        rows = DIRECT_ROWS + relay.shape[1]
        self.direct = slice(0, DIRECT_ROWS)
        self.detour = slice(DIRECT_ROWS, rows)
        self.sources = {}

    def copies(self, index):
        half, place, src = self.place.half, self.place, self.sources[index]
        near = remote(src(self.direct), self.targets(index, half, self.direct), self.send.at[index], self.recv.at[index], place.pair)
        far = remote(src(self.detour), self.relay.at[index], self.far_send.at[index], self.relay_recv.at[index], place.across)
        return near, far

    def whole(self, index):
        rows, src = slice(0, self.detour.stop), self.sources[index]
        dst = self.targets(index, self.place.half, rows)
        return remote(src(rows), dst, self.send.at[index], self.recv.at[index], self.place.pair)

    def start(self, index, src):
        self.sources[index] = src
        for copy in self.copies(index):
            copy.start()

    def start_near(self, index, src):
        self.sources[index] = src
        self.copies(index)[0].start()

    def start_far(self, index):
        self.copies(index)[1].start()

    def start_whole(self, index, src):
        self.sources[index] = src
        self.whole(index).start()

    def wait(self, index):
        other = 1 - self.place.half
        for rows, sem in ((self.direct, self.recv), (self.detour, self.far_recv)):
            dst = self.targets(index, other, rows)
            remote(dst, dst, self.send.at[index], sem.at[index], self.place.pair).wait_recv()

    def wait_whole(self, index):
        dst = self.targets(index, 1 - self.place.half, slice(0, self.detour.stop))
        remote(dst, dst, self.send.at[index], self.recv.at[index], self.place.pair).wait_recv()

    def finish(self, indices):
        for index in indices:
            for copy in self.copies(index):
                copy.wait_send()

    def finish_whole(self, indices):
        for index in indices:
            self.whole(index).wait_send()

    def forward(self, indices):
        copies = []
        for index in indices:
            held = self.relay.at[index]
            remote(held, held, self.relay_send.at[index], self.relay_recv.at[index], self.place.across).wait_recv()
            copy = remote(held, self.targets(index, self.place.half, self.detour), self.relay_send.at[index], self.far_recv.at[index], self.place.corner)
            copy.start()
            copies.append(copy)
        for copy in copies:
            copy.wait_send()


def spread(value, width):
    return jnp.broadcast_to(value, (value.shape[0], width))


def slot_block(slot):
    return (0, slot) if slot < 2 else (1, slot - 2)


def slot_weight(slot, weight):
    unit = weight.shape[1] // 8
    at = slot_block(slot)[1] * unit
    return weight[:, at:at + unit]


def mask_slot(slot, value, flag):
    if slot == 1:
        return value * (1.0 - flag)
    return value if slot < 6 else value * flag


NARROW, WIDE = (0, 1), tuple(range(2, SLOTS))
G_PLACE = (0, 1, 2, 3, 4, 5, 9, 6, 7, 8)
DG_STRAIGHT, DG_MIDDLE, DG_LATE = (0, 1, 2), (3, 4), (5, 6, 7, 8, 9)


class Sizes:
    def __init__(self, feats, cols, hidden, tokens):
        self.feats, self.cols, self.unit, self.tokens = feats, cols, hidden // 8, tokens
        self.mine, self.length, self.width = cols // 2, 2 * tokens, 2 * feats
        self.heads = self.mine // HEAD_DIM


class Saver:
    def __init__(self, sem):
        self.sem, self.copies = sem, []

    def __call__(self, src, dst):
        copy = pltpu.make_async_copy(src, dst, self.sem.at[len(self.copies)])
        copy.start()
        self.copies.append(copy)

    def finish(self):
        for copy in self.copies:
            copy.wait()


class Loader:
    def __init__(self, pairs, sem):
        self.copies = [pltpu.make_async_copy(src, dst, sem.at[n]) for n, (src, dst) in enumerate(pairs)]
        for copy in self.copies:
            copy.start()

    def wait(self, *which):
        for n in which:
            self.copies[n].wait()


class Emitter:
    def __init__(self, place, out, stage, swap, sems, first=0):
        self.place, self.out, self.stage, self.swap, self.sems, self.first = place, out, stage, swap, sems, first

    def span(self):
        feats = self.stage.shape[-1]
        return pl.ds(pl.multiple_of(self.place.half * feats, feats), feats)

    def far(self, i):
        at = self.first + i
        return remote(self.stage.at[i], self.out.at[i, :, self.span()], self.sems[0].at[at], self.sems[1].at[at], self.place.pair)

    def near(self, i):
        return pltpu.make_async_copy(self.stage.at[i], self.out.at[i, :, self.span()], self.sems[2].at[self.first + i])

    def start(self, values, owner):
        narrow, wide = (value.astype(F32) for value in values)
        self.stage[0] = (narrow * (1.0 - self.swap) + wide * self.swap).astype(BF16)
        self.stage[1] = (wide * (1.0 - self.swap) + narrow * self.swap).astype(BF16)

        @pl.when(self.place.half == owner)
        def _():
            for i in range(2):
                self.near(i).start()

        @pl.when(self.place.half != owner)
        def _():
            for i in range(2):
                self.far(i).start()

    def finish(self, owner, active=True):
        @pl.when((self.place.half == owner) & active)
        def _():
            for i in range(2):
                self.near(i).wait()
                self.far(i).wait_recv()

        @pl.when((self.place.half != owner) & active)
        def _():
            for i in range(2):
                self.far(i).wait_send()


class Gather:
    def __init__(self, place, mine, every, sems, first, last):
        self.me, self.count = lax.axis_index("dp"), lax.axis_size("dp")
        self.place, self.mine, self.every = place, mine, every
        self.right, self.left, self.recv, self.local = sems
        self.first, self.last = first, min(last, self.count - 1)

    def send(self, block, way, number):
        section, dp, mp = self.place.at
        sems = self.right if way > 0 else self.left
        src = self.mine if number == 1 else self.every.at[block]
        return remote(src, self.every.at[block], sems.at[block], self.recv.at[block], (section, dp + way, mp))

    def arrive(self, block):
        held = self.every.at[block]
        remote(held, held, self.right.at[block], self.recv.at[block], self.place.pair).wait_recv()

    def moves(self, number):
        me, last = self.me, self.count - 1
        right, left = me - number + 1, me + number - 1
        return ((1, right, (right >= 0) & (me < last)), (-1, left, (left <= last) & (me > 0)))

    def own(self):
        return pltpu.make_async_copy(self.mine, self.every.at[self.me], self.local.at[0])

    def step(self, number):
        if number == 1:
            self.own().start()
        if number > self.last:
            return
        for way, block, active in self.moves(number):
            @pl.when(active)
            def _(way=way, block=block):
                if number > self.first:
                    self.arrive(block)
                self.send(block, way, number).start()

    def rest(self, number):
        for more in range(number, self.last + 1):
            self.step(more)

    def finish(self):
        for number in range(self.first, self.last + 1):
            left, right = self.me - number, self.me + number
            done = number == self.last

            @pl.when((left >= 0) if done else (left >= 0) & (self.me == self.count - 1))
            def _(block=left):
                self.arrive(block)

            @pl.when((right < self.count) if done else (right < self.count) & (self.me == 0))
            def _(block=right):
                self.arrive(block)

            for way, block, active in self.moves(number):
                @pl.when(active)
                def _(way=way, block=block):
                    self.send(block, way, number).wait_send()
        if self.first == 1:
            self.own().wait()


def main_kernel(
    wide_ref, x0_ref, c0_ref, gain_a_ref, gain_f_ref, cos_ref, sin_ref, wqkv_hbm, wo_hbm, wu_hbm, wd_hbm,
    out_hbm, ig_hbm, q_hbm, k_hbm, v_hbm, p_hbm, xa_hbm, ra_hbm, every_hbm, every_o_hbm, every_d_hbm, every_flag_hbm, wug_hbm, dc_hbm, e_hbm, dqkv_hbm,
    gain_a_out, gain_f_out,
    wqkv, wo, wu, wd, xa, xf, x2, xg, q, k, v, p, o, ra, rf, u, g,
    own_qkv, snd_qkv, rcv_qkv, snd_u, rcv_u, snd_sq, rcv_sq, snd_br, rcv_br, rcv_half,
    e_in, e, dc, du, snd_dg, rcv_dg, dt, e_out, stage, own_do, snd_do, rcv_do, dqkv,
    snd_row, rcv_row, snd_db, rcv_db, rcv_db_half, relay,
    load_sem, x_send, x_recv, far_send, far_recv, relay_send, relay_recv, sq_send, sq_recv, core_send, core_recv,
    row_send, row_recv, db_send, db_recv, in_send, in_recv, in_local, y_send, y_recv, out_send, out_recv, out_local, save_sem,
    right_sem, left_sem, every_sem, every_local, o_right, o_left, o_sem, o_local, d_send, d_recv, d_local, flag_send, flag_recv, flag_local, wug_sem, go_sem,
):
    place = Place()
    half, core = place.half, place.core
    flag, swap = wide_ref[:1, :1], wide_ref[1:2, :1]
    seqs, length, feats = xa.shape
    z = Sizes(feats, wo.shape[1], wu.shape[1], length // 2)
    mine = z.mine

    @pl.when(place.block == 0)
    def _():
        for n, (src, dst) in enumerate(((wqkv_hbm, wqkv), (wo_hbm, wo), (wu_hbm, wu), (wd_hbm, wd))):
            pltpu.make_async_copy(src, dst, load_sem.at[n]).start()

    @pl.when(place.block == 1)
    def _():
        for n, (src, dst) in reversed(tuple(enumerate(((wqkv_hbm, wqkv), (wo_hbm, wo), (wu_hbm, wu), (wd_hbm, wd))))):
            pltpu.make_async_copy(src, dst, load_sem.at[n]).start()

    def loaded(n):
        dst = (wqkv, wo, wu, wd)[n]
        pltpu.make_async_copy(dst, dst, load_sem.at[n]).wait()

    save = Saver(save_sem)
    place.barrier()

    first_u, first_dg = 6 + seqs, 6 + seqs + SLOTS
    first_do = first_dg + SLOTS

    def targets(index, sender_half, rows):
        span = pl.ds(pl.multiple_of(sender_half * mine, mine), mine)
        if index < 6:
            return rcv_qkv.at[index // 3, index % 3, rows, :]
        if index < first_u:
            return o.at[index - 6, rows, span]
        if index < first_dg:
            return rcv_u.at[index - first_u, rows, :]
        if index < first_do:
            return rcv_dg.at[index - first_dg, rows, :]
        if index < first_do + seqs:
            return rcv_do.at[index - first_do, rows, :]
        n = index - first_do - seqs
        return dqkv.at[n // 3, n % 3, rows, span]

    link = PairLink(place, relay, (x_send, x_recv, far_send, far_recv, relay_send, relay_recv), targets)
    forward_order = tuple(range(first_dg))
    ffn_order = tuple(range(first_dg, first_do))
    attn_order = tuple(range(first_do, first_do + seqs + 6))
    my_rows = pl.ds(pl.multiple_of(core * z.tokens, z.tokens), z.tokens)
    their_rows = pl.ds(pl.multiple_of((1 - core) * z.tokens, z.tokens), z.tokens)
    my_feats = pl.ds(pl.multiple_of(half * feats, feats), feats)
    gather = Gather(place, g.at[0:SLOTS - 1], every_hbm, (right_sem, left_sem, every_sem, every_local), 1, EARLY_STEPS)
    gather_o = Gather(place, o, every_o_hbm, (o_right, o_left, o_sem, o_local), 1, z.length)
    share = feats // lax.axis_size("dp")

    def dt_rows(n):
        return dt.at[pl.ds(pl.multiple_of(n * share, share), share), :]

    exchange_d = Exchange(place, dt_rows, every_d_hbm, (d_send, d_recv, d_local))
    exchange_flag = Exchange(place, lambda n: wide_ref, every_flag_hbm, (flag_send, flag_recv, flag_local))
    exchange_flag.start()

    def local_copy(src, dst, n):
        return pltpu.make_async_copy(src, dst, in_local.at[n])

    def core_half(src, dst, n):
        return remote(src, dst, in_send.at[n], in_recv.at[n], place.core_peer)

    def x_copy(i):
        return remote(x2.at[i], xa.at[i, my_rows, :], y_send.at[i], y_recv.at[i], place.across)

    def e_copy(i):
        return remote(e_out.at[i], e_in.at[i, my_rows, :], y_send.at[i], y_recv.at[i], place.across)

    def start_half(src_ref, dst_ref, first):
        for i in range(seqs):
            local_copy(src_ref.at[i, :, my_feats], dst_ref.at[i, my_rows, :], first + i).start()
            core_half(src_ref.at[i, :, my_feats], dst_ref.at[i, my_rows, :], first + i).start()

    def ordered_halves(raw_ref, dst_ref, first):
        for i in range(seqs):
            local_copy(raw_ref.at[i, my_rows, :], raw_ref.at[i, my_rows, :], first + i).wait()
            core_half(raw_ref.at[i, my_rows, :], raw_ref.at[i, my_rows, :], first + i).wait()
        for i in range(seqs):
            mixed = raw_ref[i].astype(F32) * (1.0 - swap) + raw_ref[1 - i].astype(F32) * swap
            dst_ref[i] = mixed.astype(BF16)

    def pass_half(dst_ref, n, i):
        core_half(dst_ref.at[i, my_rows, :], dst_ref.at[i, my_rows, :], n).start()
        core_half(dst_ref.at[i, my_rows, :], dst_ref.at[i, my_rows, :], n).wait()

    def sq_copy(n):
        return remote(snd_sq.at[n], rcv_sq.at[n], sq_send.at[n], sq_recv.at[n], place.pair)

    def core_copy(n):
        return remote(snd_br.at[n], rcv_br.at[n], core_send.at[n], core_recv.at[n], place.core_peer)

    def core_rows(i):
        return remote(snd_br.at[2 + i, their_rows, :], rcv_half.at[i], core_send.at[2 + i], core_recv.at[2 + i], place.core_peer)

    def row_copy(n, peer):
        return remote(snd_row.at[n], rcv_row.at[n], row_send.at[n], row_recv.at[n], peer)

    def db_copy(n):
        return remote(snd_db.at[n], rcv_db.at[n], db_send.at[n], db_recv.at[n], place.core_peer)

    out_sems = (out_send, out_recv, out_local)
    def ready(n):
        pl.semaphore_signal(go_sem.at[n], inc=1, device_id=place.pair, device_id_type=MESH)

    def wait_ready(n):
        pl.semaphore_wait(go_sem.at[n], 1)

    emit_x1 = Emitter(place, out_hbm, stage.at[0], swap, out_sems, 0)
    emit_x2 = Emitter(place, out_hbm, stage.at[1], swap, out_sems, 2)
    emit_e1 = Emitter(place, ig_hbm, stage.at[2], swap, out_sems, 4)
    emit_e0 = Emitter(place, ig_hbm, stage.at[3], swap, out_sems, 6)
    theirs = pl.multiple_of((1 - half) * mine, mine)
    ours = pl.multiple_of(half * mine, mine)
    gain_a, gain_f = gain_a_ref[...], gain_f_ref[...]

    def dg_part(slot):
        snd_dg[slot] = mm(e_in[slot_block(slot)[0]], slot_weight(slot, wd)).astype(BF16)

    @pl.when(place.block == 0)
    def _():
        start_half(x0_ref, xf, 0)
        ordered_halves(xf, xa, 0)

    @pl.when(place.block == 1)
    def _():
        start_half(c0_ref, dc, 2)
        loaded(3)
        ordered_halves(dc, e_in, 2)
        for slot in range(SLOTS):
            dg_part(slot)
        for i in range(seqs):
            dt[:, i * length:(i + 1) * length] = jnp.transpose(e_in[i].astype(F32)).astype(BF16)
        exchange_d.start()
        link.forward(forward_order[:6])
        link.start_whole(first_dg, lambda rows: snd_dg.at[0, rows, :])
        link.forward(forward_order[6:8])
        link.start_whole(first_dg + 1, lambda rows: snd_dg.at[1, rows, :])
        link.forward(forward_order[8:])
        link.start_whole(first_dg + 2, lambda rows: snd_dg.at[2, rows, :])

    for i in range(seqs):
        @pl.when(place.block == 1)
        def _():
            x_copy(i).wait_recv()
            if i == 1:
                ready(0)
            pass_half(xa, i, i)

        x = xa[i].astype(F32)
        snd_sq[i] = to_row(jnp.sum(x * x, axis=-1, keepdims=True))
        sq_copy(i).start()
        xg[i] = (x * gain_a).astype(BF16)
        if i == 0:
            loaded(0)
        for t in range(3):
            snd_qkv[i, t] = mm(xg[i], wqkv[t, :, pl.ds(theirs, mine)]).astype(BF16)
            source = lambda rows, i=i, t=t: snd_qkv.at[i, t, rows, :]

            @pl.when(place.block == 0)
            def _():
                link.start(3 * i + t, source)

            @pl.when(place.block == 1)
            def _():
                if i == 0:
                    link.start_whole(t, source)
                else:
                    link.start_near(3 + t, source)
    @pl.when(place.block == 1)
    def _():
        wait_ready(0)
        for t in range(3):
            link.start_far(3 + t)

    for i in range(seqs):
        for t in range(3):
            own_qkv[i, t] = mm(xg[i], wqkv[t, :, pl.ds(ours, mine)])

    cosine, sine = cos_ref[...], sin_ref[...]
    scale = HEAD_DIM ** (-0.5)
    causal = lax.broadcasted_iota(jnp.int32, (length, length), 0) >= lax.broadcasted_iota(jnp.int32, (length, length), 1)
    for i in range(seqs):
        sq_copy(i).wait_recv()
        factor = lax.rsqrt((from_row(snd_sq[i]) + from_row(rcv_sq[i])) * (1.0 / z.width) + EPSILON)
        ra[i] = spread(factor, 128)
        if i == 0:
            @pl.when(place.block == 0)
            def _():
                for t in range(3):
                    link.wait(t)

            @pl.when(place.block == 1)
            def _():
                for t in range(3):
                    link.wait_whole(t)
        else:
            for t in range(3):
                link.wait(3 + t)
        for j in range(z.heads):
            span = pl.ds(j * HEAD_DIM, HEAD_DIM)
            raw = [(own_qkv[i, t, :, span] + rcv_qkv[i, t, :, span].astype(F32)) * factor for t in range(3)]
            q_j = (raw[0] * cosine + turned(raw[0]) * sine).astype(BF16)
            k_j = (raw[1] * cosine + turned(raw[1]) * sine).astype(BF16)
            v_j = raw[2].astype(BF16)
            q[i, :, span], k[i, :, span], v[i, :, span] = q_j, k_j, v_j
            scores = jnp.where(causal, mm_nt(q_j, k_j) * scale, -1e30)
            exponent = jnp.exp(scores - jnp.max(scores, axis=-1, keepdims=True))
            probs = exponent / jnp.sum(exponent, axis=-1, keepdims=True)
            p[i, j] = probs
            o[i, :, pl.ds(pl.multiple_of(ours + j * HEAD_DIM, HEAD_DIM), HEAD_DIM)] = mm(probs.astype(BF16), v_j).astype(BF16)
        link.start(6 + i, lambda rows, i=i: o.at[i, rows, pl.ds(ours, mine)])

    loaded(1)
    for i in range(seqs):
        link.wait(6 + i)
        snd_br[i] = mm_nt(o[i], wo[...]).astype(BF16)
        core_copy(i).start()

    @pl.when(place.block == 1)
    def _():
        for slot in DG_MIDDLE:
            link.start(first_dg + slot, lambda rows, slot=slot: snd_dg.at[slot, rows, :])

    gather_o.step(1)

    def slot_start(slot):
        part = mm(xg[slot_block(slot)[0]], slot_weight(slot, wu))
        u[slot] = part
        snd_u[slot] = part.astype(BF16)
        link.start(first_u + slot, lambda rows: snd_u.at[slot, rows, :])

    loaded(2)
    for i, slots in enumerate((NARROW, WIDE)):
        core_copy(i).wait_recv()
        xf[i] = (xa[i].astype(F32) + (snd_br[i].astype(F32) + rcv_br[i].astype(F32))).astype(BF16)
        x = xf[i].astype(F32)
        snd_sq[2 + i] = to_row(jnp.sum(x * x, axis=-1, keepdims=True))
        sq_copy(2 + i).start()
        xg[i] = (x * gain_f).astype(BF16)
        for slot in slots:
            slot_start(slot)

    @pl.when(place.block == 1)
    def _():
        for slot in DG_LATE:
            link.start(first_dg + slot, lambda rows, slot=slot: snd_dg.at[slot, rows, :])

    emit_x1.start([xf[i, my_rows, :] for i in range(seqs)], 0)

    for ref, dst in ((q, q_hbm), (k, k_hbm), (v, v_hbm), (p, p_hbm), (xa, xa_hbm), (ra, ra_hbm)):
        save(ref, dst)

    factors = {}

    def row_factor(i):
        sq_copy(2 + i).wait_recv()
        factors[i] = lax.rsqrt((from_row(snd_sq[2 + i]) + from_row(rcv_sq[2 + i])) * (1.0 / z.width) + EPSILON)
        rf[i] = spread(factors[i], 128)

    def activate(slot):
        link.wait(first_u + slot)
        value = (u[slot] + rcv_u[slot].astype(F32)) * factors[slot_block(slot)[0]]
        u[slot] = value
        active = 0.5 * value * (1.0 + jnp.tanh(GELU_C * (value + GELU_A * (value * value * value))))
        g_k = mask_slot(slot, active, flag).astype(BF16)
        g[G_PLACE[slot]] = g_k
        return mm_nt(g_k, slot_weight(slot, wd))

    def finish_rows(i):
        core_rows(i).wait_recv()
        x2[i] = (xf[i, my_rows, :].astype(F32) + (snd_br[2 + i, my_rows, :].astype(F32) + rcv_half[i].astype(F32))).astype(BF16)

        @pl.when(place.block == 0)
        def _():
            x_copy(i).start()

    @pl.when(place.block == 0)
    def _():
        loaded(3)

    row_factor(0)
    snd_br[2] = (activate(0) + activate(1)).astype(BF16)
    core_rows(0).start()
    gather_o.step(2)
    row_factor(1)
    total = activate(2) + activate(3)
    finish_rows(0)
    for slot in WIDE[2:]:
        total = total + activate(slot)
    snd_br[3] = total.astype(BF16)
    core_rows(1).start()
    g[1] = g[1] + g[SLOTS - 1]
    finish_rows(1)
    emit_x2.start([x2[i] for i in range(seqs)], 1)
    gather.step(1)
    gather_o.rest(3)

    def slope_of(value):
        squared = value * value
        bent = jnp.tanh(GELU_C * (value + GELU_A * (squared * value)))
        return 0.5 * (1.0 + bent) + 0.5 * value * (1.0 - bent * bent) * (GELU_C * (1.0 + 3.0 * GELU_A * squared))

    @pl.when(place.block == 0)
    def _():
        link.forward(forward_order[3:first_u])
        link.forward(tuple(first_dg + slot for slot in DG_MIDDLE))
        link.forward(forward_order[first_u:])
        gather.step(2)
        link.forward(tuple(first_dg + slot for slot in DG_LATE))
        link.forward(attn_order)
        for i, slots in enumerate((NARROW, WIDE)):
            e_copy(i).wait_recv()
            if i == 1:
                ready(1)
            pass_half(e_in, 2 + i, i)
            for slot in slots:
                dg_part(slot)
                source = lambda rows, slot=slot: snd_dg.at[slot, rows, :]
                if i == 0:
                    link.start_whole(first_dg + slot, source)
                else:
                    link.start_near(first_dg + slot, source)
                if i == 1 and slot == WIDE[1]:
                    wait_ready(1)
                    for sent in WIDE[:2]:
                        link.start_far(first_dg + sent)
                if i == 1 and slot > WIDE[1]:
                    link.start_far(first_dg + slot)
        for i in range(seqs):
            dt[:, i * length:(i + 1) * length] = jnp.transpose(e_in[i].astype(F32)).astype(BF16)
        exchange_d.start()

    def hidden_back(slot):
        @pl.when(place.block == 0)
        def _():
            (link.wait_whole if slot in NARROW else link.wait)(first_dg + slot)

        @pl.when(place.block == 1)
        def _():
            (link.wait_whole if slot in DG_STRAIGHT else link.wait)(first_dg + slot)

        value = u[slot]
        grad = snd_dg[slot].astype(F32) + rcv_dg[slot].astype(F32)
        du_k = mask_slot(slot, grad * slope_of(value), flag).astype(BF16)
        du[slot] = du_k
        return mm_nt(du_k, slot_weight(slot, wu)), jnp.sum(du_k.astype(F32) * value, axis=-1, keepdims=True)

    def wug_copy(block):
        return pltpu.make_async_copy(snd_qkv.at[block % 2], wug_hbm.at[:, :, block * z.unit:(block + 1) * z.unit], wug_sem.at[block % 2])

    def up_grad(block):
        part = mm_tn(xg[1], du[2 + block])
        if block < 2:
            part = part + mm_tn(xg[0], du[block])
        if block >= 2:
            wug_copy(block - 2).wait()
        for t in range(3):
            snd_qkv[block % 2, t] = part[t * length:(t + 1) * length].astype(BF16)
        wug_copy(block).start()

    def core_sum_start(i, slots):
        total = row = None
        for slot in slots:
            more, more_row = hidden_back(slot)
            total, row = (more, more_row) if total is None else (total + more, row + more_row)

            if i == 1:
                @pl.when(place.block == 0)
                def _(slot=slot):
                    up_grad(slot - 2)

        snd_db[i] = total.astype(BF16)
        db_copy(i).start()
        snd_row[i] = to_row(row)
        row_copy(i, place.core_peer).start()

    def ffn_done(i):
        db_copy(i).wait_recv()
        row_copy(i, place.core_peer).wait_recv()
        mean = (from_row(snd_row[i]) + from_row(rcv_row[i])) * (1.0 / z.width)
        grad = snd_db[i].astype(F32) + rcv_db[i].astype(F32)
        factor = rf[i][:, :1]
        scaled = xf[i].astype(F32) * factor
        new = e_in[i].astype(F32) + factor * (grad * gain_f - scaled * mean)
        e[i] = new
        dc[i] = new.astype(BF16)
        return jnp.sum(grad * scaled, axis=0, keepdims=True)

    @pl.when(place.block == 0)
    def _():
        link.finish(forward_order[:3])

    @pl.when(place.block == 1)
    def _():
        link.finish_whole(forward_order[:3])

    link.finish(forward_order[3:6])
    for i in range(seqs):
        xg[i] = (xf[i].astype(F32) * rf[i][:, :1] * gain_f).astype(BF16)
    core_sum_start(0, NARROW)
    gain_total = ffn_done(0)

    @pl.when(place.block == 1)
    def _():
        attention_grad_start(0, dc, wo, own_do, snd_do, link, first_do, theirs, ours, mine)

    core_sum_start(1, WIDE)
    gain_total = gain_total + ffn_done(1)
    gain_f_out[...] = jnp.broadcast_to(gain_total, gain_f_out.shape)

    @pl.when(place.block == 1)
    def _():
        attention_grad_start(1, dc, wo, own_do, snd_do, link, first_do, theirs, ours, mine)

    save(dc, dc_hbm)
    save(e, e_hbm)
    emit_e1.start([dc[i, my_rows, :] for i in range(seqs)], 1)

    @pl.when(place.block == 0)
    def _():
        gain_a_out[...] = jnp.zeros_like(gain_a_out)

    @pl.when(place.block == 1)
    def _():
        attention_grad(
            place, z, seqs, e, cosine, sine, gain_a, wqkv, q, k, v, p, xa, ra, own_do, rcv_do, dqkv,
            snd_row, rcv_row, row_copy, 2, snd_db, rcv_db_half, db_send, db_recv, 2, link, first_do,
            my_rows, their_rows, ours, mine, e_out, gain_a_out, emit_e0, e_copy,
        )
        copy = pltpu.make_async_copy(dqkv, dqkv_hbm, in_local.at[4])
        copy.start()
        gather.step(2)
        link.forward(ffn_order[len(NARROW):])
        for block in range(8):
            up_grad(block)
        copy.wait()

    for block in range(6, 8):
        wug_copy(block).wait()
    link.finish(forward_order[6:])
    for n in range(4):
        sq_copy(n).wait_send()
    for i in range(seqs):
        core_copy(i).wait_send()
        core_rows(i).wait_send()
        row_copy(i, place.core_peer).wait_send()
        db_copy(i).wait_send()

    @pl.when(place.block == 0)
    def _():
        link.finish_whole(ffn_order[:len(NARROW)])
        link.finish(ffn_order[len(NARROW):])
        for i in range(seqs):
            x_copy(i).wait_send()

    @pl.when(place.block == 1)
    def _():
        link.finish_whole(tuple(first_dg + slot for slot in DG_STRAIGHT))
        link.finish(tuple(first_dg + slot for slot in DG_MIDDLE + DG_LATE))
        link.finish(attn_order)
        for n in range(2, 6):
            row_copy(n, place.core_peer).wait_send()
        for i in range(seqs):
            half_copy(place, snd_db, rcv_db_half, db_send, db_recv, 2, i, their_rows).wait_send()
            e_copy(i).wait_send()

    emit_x1.finish(0)
    emit_x2.finish(1)
    emit_e1.finish(1)
    emit_e0.finish(0, place.block == 1)
    exchange_d.finish()
    exchange_flag.finish()
    gather.finish()
    gather_o.finish()
    save.finish()


def half_copy(place, snd_br, rcv_half, core_send, core_recv, first, i, their_rows):
    at = first + i
    return remote(snd_br.at[at, their_rows, :], rcv_half.at[i], core_send.at[at], core_recv.at[at], place.core_peer)


def attention_grad_start(i, dc, wo, own_do, snd_do, link, first, theirs, ours, mine):
    snd_do[i] = mm(dc[i], wo[:, pl.ds(theirs, mine)]).astype(BF16)
    link.start(first + i, lambda rows: snd_do.at[i, rows, :])
    own_do[i] = mm(dc[i], wo[:, pl.ds(ours, mine)])


def attention_grad(
    place, z, seqs, e, cosine, sine, gain_a, wqkv, q, k, v, p, xa, ra, own_do, rcv_do, dqkv,
    snd_row, rcv_row, row_copy, row_first, snd_br, rcv_half, core_send, core_recv, core_first, link, first,
    my_rows, their_rows, ours, mine, e_out, gain_a_out, emit, y_copy, between=None,
):
    length, feats = z.length, z.feats
    scale = HEAD_DIM ** (-0.5)
    for i in range(seqs):
        link.wait(first + i)
        row = jnp.zeros((length, 1), F32)
        for j in range(z.heads):
            span = pl.ds(j * HEAD_DIM, HEAD_DIM)
            do_j = (own_do[i, :, span] + rcv_do[i, :, span].astype(F32)).astype(BF16)
            q_j, k_j, v_j, probs = q[i, :, span], k[i, :, span], v[i, :, span], p[i, j]
            dp = mm_nt(do_j, v_j)
            dv = mm_tn(probs.astype(BF16), do_j)
            ds = (probs * (dp - jnp.sum(probs * dp, axis=-1, keepdims=True))).astype(BF16)
            dq = mm(ds, k_j) * scale
            dk = mm_tn(ds, q_j) * scale
            row = row + jnp.sum(dq * q_j.astype(F32) + dk * k_j.astype(F32) + dv * v_j.astype(F32), axis=-1, keepdims=True)
            at = pl.ds(pl.multiple_of(ours + j * HEAD_DIM, HEAD_DIM), HEAD_DIM)
            dqkv[i, 0, :, at] = (dq * cosine - turned(dq) * sine).astype(BF16)
            dqkv[i, 1, :, at] = (dk * cosine - turned(dk) * sine).astype(BF16)
            dqkv[i, 2, :, at] = dv.astype(BF16)
        snd_row[row_first + i] = to_row(row)
        row_copy(row_first + i, place.pair).start()
        for t in range(3):
            link.start(first + seqs + 3 * i + t, lambda rows, i=i, t=t: dqkv.at[i, t, rows, pl.ds(ours, mine)])

    if between is not None:
        between()
    for i in range(seqs):
        part = jnp.zeros((length, feats), F32)
        for t in range(3):
            link.wait(first + seqs + 3 * i + t)
            part = part + mm_nt(dqkv[i, t], wqkv[t])
        snd_br[core_first + i] = part.astype(BF16)
        half_copy(place, snd_br, rcv_half, core_send, core_recv, core_first, i, their_rows).start()
        row_copy(row_first + i, place.pair).wait_recv()
        snd_row[row_first + 2 + i] = snd_row[row_first + i] + rcv_row[row_first + i]
        row_copy(row_first + 2 + i, place.core_peer).start()

    gain_total = jnp.zeros((1, feats), F32)
    for i in range(seqs):
        half_copy(place, snd_br, rcv_half, core_send, core_recv, core_first, i, their_rows).wait_recv()
        row_copy(row_first + 2 + i, place.core_peer).wait_recv()
        mean = (from_row(snd_row[row_first + 2 + i]) + from_row(rcv_row[row_first + 2 + i])) * (1.0 / z.width)
        snd_row[row_first + 4 + i] = to_row(mean)
        own_mean = from_row(snd_row[row_first + 4 + i, :, my_rows])
        grad = snd_br[core_first + i, my_rows, :].astype(F32) + rcv_half[i].astype(F32)
        factor = ra[i, my_rows, :][:, :1]
        scaled = xa[i, my_rows, :].astype(F32) * factor
        e_out[i] = (e[i, my_rows, :] + factor * (grad * gain_a - scaled * own_mean)).astype(BF16)
        gain_total = gain_total + jnp.sum(grad * scaled, axis=0, keepdims=True)
        if y_copy is not None:
            y_copy(i).start()
    emit.start([e_out[i] for i in range(seqs)], 0)
    gain_a_out[...] = jnp.broadcast_to(gain_total, gain_a_out.shape)


def last_kernel(
    wide_ref, e_hbm, dc_hbm, gain_a_ref, gain_a_in, gain_f_in, cos_ref, sin_ref, wqkv_hbm, wo_hbm, q_hbm, k_hbm, v_hbm, p_hbm,
    xa_hbm, ra_hbm, dqkv_hbm, every_o_hbm, every_d_hbm, every_flag_hbm, every_in, ig_in,
    ig_hbm, every_hbm, qkv_out, wo_out, wd_out, gains_out,
    e, dc, wqkv, wo, q, k, v, p, xa, ra, ab,
    own_do, snd_do, rcv_do, dqkv, e_out, stage, snd_row, rcv_row, snd_br, rcv_half, relay,
    dct, every_c, mine_grad, from_left, from_right, block_g, block_o, block_d, flags, wd_sum, wo_sum, gains, core_gains, every_gain, gain_a_new,
    load_sem, x_send, x_recv, far_send, far_recv, relay_send, relay_recv, row_send, row_recv, core_send, core_recv,
    out_send, out_recv, out_local, right_sem, left_sem, every_sem, c_send, c_recv, c_local, gain_send, gain_recv, gain_local,
    pair_send, pair_recv, scatter_right, scatter_left, got_left, got_right, block_sem, out_sem,
):
    place = Place()
    half, core = place.half, place.core
    swap = wide_ref[1:2, :1]
    seqs, length, feats = xa.shape
    z = Sizes(feats, wo.shape[1], 8, length // 2)
    mine = z.mine
    me, planes = lax.axis_index("dp"), lax.axis_size("dp")
    share = feats // planes
    sources = (dc_hbm, wo_hbm, q_hbm, k_hbm, v_hbm, p_hbm, wqkv_hbm, e_hbm, xa_hbm, ra_hbm, every_flag_hbm)
    loads = Loader(tuple(zip(sources, (dc, wo, q, k, v, p, wqkv, e, xa, ra, flags))), load_sem)
    place.barrier()

    def targets(index, sender_half, rows):
        if index < seqs:
            return rcv_do.at[index, rows, :]
        n = index - seqs
        return dqkv.at[n // 3, n % 3, rows, pl.ds(pl.multiple_of(sender_half * mine, mine), mine)]

    link = PairLink(place, relay, (x_send, x_recv, far_send, far_recv, relay_send, relay_recv), targets)
    my_rows = pl.ds(pl.multiple_of(core * z.tokens, z.tokens), z.tokens)
    their_rows = pl.ds(pl.multiple_of((1 - core) * z.tokens, z.tokens), z.tokens)
    theirs = pl.multiple_of((1 - half) * mine, mine)
    ours = pl.multiple_of(half * mine, mine)
    emit = Emitter(place, ig_hbm, stage, swap, (out_send, out_recv, out_local))

    def row_copy(n, peer):
        return remote(snd_row.at[n], rcv_row.at[n], row_send.at[n], row_recv.at[n], peer)

    held = pltpu.make_async_copy(dqkv_hbm, dqkv, load_sem.at[11])
    gather = Gather(place, every_hbm.at[0], every_hbm, (right_sem, left_sem, every_sem, None), EARLY_STEPS + 1, z.length)
    gather.rest(EARLY_STEPS + 1)

    def share_rows(n):
        return pl.ds(pl.multiple_of(n * share, share), share)

    exchange_c = Exchange(place, lambda n: dct.at[share_rows(n), :], every_c, (c_send, c_recv, c_local))

    def normed():
        for i in range(seqs):
            ab[i] = (xa[i].astype(F32) * ra[i][:, :1] * gain_a_ref[...]).astype(BF16)

    def exchange_dc():
        for i in range(seqs):
            dct[:, i * length:(i + 1) * length] = jnp.transpose(dc[i].astype(F32)).astype(BF16)
        exchange_c.start()

    def fetch(src, dst, n):
        copy = pltpu.make_async_copy(src, dst, block_sem.at[n])
        copy.start()
        return copy

    def plane_down(n):
        copies = [fetch(every_hbm.at[n], block_g, 0), fetch(every_d_hbm.at[n], block_d, 1)]
        for copy in copies:
            copy.wait()
        flag = flags[n][:1, :1]
        shared = block_g[1].astype(F32)
        upper, lower = (shared * flag).astype(BF16), (shared * (1.0 - flag)).astype(BF16)
        narrow, wide = block_d[:, :length], block_d[:, length:]
        unit = block_g.shape[2]
        for block in range(8):
            right = upper if block == 4 else block_g[2 + block if block < 4 else 1 + block]
            part = mm(wide, right)
            if block < 2:
                part = part + mm(narrow, block_g[0] if block == 0 else lower)
            span = slice(block * unit, (block + 1) * unit)
            wd_sum[:, span] = wd_sum[:, span] + part

    def far(n):
        return (n - me > EARLY_STEPS) | (me - n > EARLY_STEPS)

    def down_grad(late):
        def body(n, carry):
            @pl.when(far(n) if late else jnp.logical_not(far(n)))
            def _():
                plane_down(n)
            return carry
        lax.fori_loop(0, planes, body, 0)

    def out_grad():
        def body(n, carry):
            fetch(every_o_hbm.at[n], block_o, 0).wait()
            wo_sum[...] = wo_sum[...] + mm(every_c[n][:, :length], block_o[0]) + mm(every_c[n][:, length:], block_o[1])
            return carry
        lax.fori_loop(0, planes, body, 0)

    def scatter(target, t, way):
        edge = me == (0 if way > 0 else planes - 1)
        got, sem_in = (from_left, got_left) if way > 0 else (from_right, got_right)
        sems = scatter_right if way > 0 else scatter_left
        own = mine_grad.at[t, share_rows(target), :]
        slot = got.at[target, t]
        at = target * 3 + t
        section, dp, mp = place.at
        peer = (section, dp + way, mp)

        @pl.when((me < target) if way > 0 else (me > target))
        def _():
            @pl.when(edge)
            def _():
                remote(own, slot, sems.at[at], sem_in.at[at], peer).start()

            @pl.when(jnp.logical_not(edge))
            def _():
                remote(slot, slot, sems.at[at], sem_in.at[at], place.pair).wait_recv()
                got[target, t] = (got[target, t].astype(F32) + mine_grad[t, share_rows(target), :].astype(F32)).astype(BF16)
                remote(slot, slot, sems.at[at], sem_in.at[at], peer).start()

    def scatter_end(target, t, way):
        slot = (from_left if way > 0 else from_right).at[target, t]
        at = target * 3 + t

        @pl.when((me < target) if way > 0 else (me > target))
        def _():
            sems, sem_in = (scatter_right, got_left) if way > 0 else (scatter_left, got_right)
            remote(slot, slot, sems.at[at], sem_in.at[at], place.pair).wait_send()

    def scatter_last(t):
        at = me * 3 + t
        total = mine_grad[t, share_rows(me), :].astype(F32)

        @pl.when(me > 0)
        def _():
            slot = from_left.at[me, t]
            remote(slot, slot, scatter_right.at[at], got_left.at[at], place.pair).wait_recv()

        @pl.when(me < planes - 1)
        def _():
            slot = from_right.at[me, t]
            remote(slot, slot, scatter_left.at[at], got_right.at[at], place.pair).wait_recv()

        qkv_sum = total
        left = jnp.where(me > 0, 1.0, 0.0)
        right = jnp.where(me < planes - 1, 1.0, 0.0)
        qkv_out[t] = qkv_sum + from_left[me, t].astype(F32) * left + from_right[me, t].astype(F32) * right

    for ref in (wd_sum, wo_sum):
        ref[...] = jnp.zeros_like(ref)

    @pl.when(me == 0)
    def _():
        from_left[0] = jnp.zeros_like(from_left[0])

    @pl.when(me == planes - 1)
    def _():
        from_right[planes - 1] = jnp.zeros_like(from_right[planes - 1])

    @pl.when(place.block == 1)
    def _():
        held.start()
        loads.wait(*range(11))
        held.wait()
        gain_a_new[...] = gain_a_in[...]
        exchange_dc()
        link.forward(tuple(range(seqs + 6)))
        normed()

    @pl.when(place.block == 0)
    def _():
        loads.wait(0, 1)
        for i in range(seqs):
            attention_grad_start(i, dc, wo, own_do, snd_do, link, 0, theirs, ours, mine)
        loads.wait(*range(2, 11))
        exchange_dc()

        def between():
            normed()
            down_grad(False)

        attention_grad(
            place, z, seqs, e, cos_ref[...], sin_ref[...], gain_a_ref[...], wqkv, q, k, v, p, xa, ra, own_do, rcv_do, dqkv,
            snd_row, rcv_row, row_copy, 0, snd_br, rcv_half, core_send, core_recv, 0, link, 0,
            my_rows, their_rows, ours, mine, e_out, gain_a_new, emit, None, between,
        )

    for t in range(3):
        mine_grad[t] = (mm_tn(ab[0], dqkv[0, t]) + mm_tn(ab[1], dqkv[1, t])).astype(BF16)
        if t == 0:
            gains[0:8, :] = jnp.concatenate([gain_a_new[0:1, :], 0.5 * gain_f_in[0:1, :], jnp.zeros_like(gain_a_new[0:6, :])], axis=0)
            pair_gains = remote(gains, core_gains, pair_send.at[0], pair_recv.at[0], place.core_peer)
            pair_gains.start()
        scatter(planes - 1, t, 1)
        scatter(0, t, -1)
    pair_gains.wait()
    every_gain[me] = gains[...] + core_gains[...]
    exchange_gain = Exchange(place, lambda n: every_gain.at[me], every_gain, (gain_send, gain_recv, gain_local))
    for n in range(1, planes):
        exchange_gain.copy(n).start()

    @pl.when(place.block == 1)
    def _():
        down_grad(False)

    for n in range(1, planes - 1):
        for t in range(3):
            scatter(planes - 1 - n, t, 1)
            scatter(n, t, -1)
    exchange_c.finish()
    out_grad()
    wo_copy = pltpu.make_async_copy(wo_sum, wo_out, out_sem.at[0])
    wo_copy.start()
    gather.finish()
    down_grad(True)
    wd_copy = pltpu.make_async_copy(wd_sum, wd_out, out_sem.at[1])
    wd_copy.start()
    for n in range(1, planes):
        source = lax.rem(me + planes - n, planes)
        slot = every_gain.at[source]
        remote(slot, slot, gain_send.at[n], gain_recv.at[n], place.pair).wait_recv()
        exchange_gain.copy(n).wait_send()
    total = every_gain[0]
    for n in range(1, planes):
        total = total + every_gain[n]
    gains_out[...] = total
    for t in range(3):
        scatter_last(t)
    for n in range(planes - 1):
        for t in range(3):
            scatter_end(planes - 1 - n, t, 1)
            scatter_end(n, t, -1)
    wo_copy.wait()
    wd_copy.wait()

    @pl.when(place.block == 0)
    def _():
        link.finish(tuple(range(seqs + 6)))
        for n in range(4):
            row_copy(n, place.core_peer).wait_send()
        for i in range(seqs):
            half_copy(place, snd_br, rcv_half, core_send, core_recv, 0, i, their_rows).wait_send()

    emit.finish(0, place.block == 0)


def shape(dims, kind):
    return jax.ShapeDtypeStruct(dims, kind)


ANY = pl.BlockSpec(memory_space=pl.ANY)
IN_VMEM = pl.BlockSpec(memory_space=pltpu.VMEM)


def vmem(dims, kind):
    return pltpu.VMEM(tuple(dims), kind)


def dma(*counts):
    return [pltpu.SemaphoreType.DMA((count,)) for count in counts]


def like(*arrays):
    return [vmem(array.shape, array.dtype) for array in arrays]


def call(kernel, name, number, out_shape, in_vmem, out_vmem, scratch, args, flops, aliases={}):
    return pl.pallas_call(
        kernel,
        out_shape=tuple(out_shape),
        in_specs=[IN_VMEM if n in in_vmem else ANY for n in range(len(args))],
        out_specs=tuple(IN_VMEM if n in out_vmem else ANY for n in range(len(out_shape))),
        scratch_shapes=scratch,
        compiler_params=pltpu.CompilerParams(collective_id=number, has_side_effects=True, vmem_limit_bytes=VMEM_LIMIT),
        cost_estimate=pl.CostEstimate(flops=flops, bytes_accessed=10**6, transcendentals=0),
        input_output_aliases=aliases,
        name=name,
    )(*args)


def run_main(wide, x0, c0, gain_a, gain_f, cosine, sine, wqkv, wo, wu, wd):
    seqs, tokens, width = x0.shape
    planes = lax.axis_size("dp")
    z = Sizes(wo.shape[0], wo.shape[1], wu.shape[1], tokens)
    state, half_state, heads_state = (seqs, z.length, z.feats), (seqs, tokens, z.feats), (seqs, z.length, z.mine)
    scores, slots = (seqs, z.heads, z.length, z.length), (SLOTS, z.length, z.unit)
    qkv, dqkv, messages = (seqs, 3, z.length, z.mine), (seqs, 3, z.length, z.cols), 12 + 2 * seqs + 2 * SLOTS
    gain, row = shape((8, z.feats), F32), (seqs, z.length, 128)
    out_shape = [shape((seqs, tokens, width), BF16)] * 2 + [shape(heads_state, BF16)] * 3 + [
        shape(scores, F32), shape(state, BF16), shape(row, F32), shape((planes, SLOTS - 1, z.length, z.unit), BF16),
        shape((planes, seqs, z.length, z.cols), BF16), shape((planes, z.feats // planes, seqs * z.length), BF16),
        shape((planes, 8, 128), F32),
        shape((3, z.length, wu.shape[1]), BF16),
        shape(state, BF16), shape(state, F32), shape(dqkv, BF16), gain, gain,
    ]
    small = (8, 8, z.length)
    scratch = like(wqkv, wo, wu, wd) + [
        vmem(state, BF16), vmem(state, BF16), vmem(half_state, BF16), vmem(state, BF16),
        vmem(heads_state, BF16), vmem(heads_state, BF16), vmem(heads_state, BF16), vmem(scores, F32),
        vmem((seqs, z.length, z.cols), BF16), vmem(row, F32), vmem(row, F32), vmem(slots, F32), vmem(slots, BF16),
        vmem(qkv, F32), vmem(qkv, BF16), vmem(qkv, BF16), vmem(slots, BF16), vmem(slots, BF16),
        vmem((4, 8, z.length), F32), vmem((4, 8, z.length), F32),
        vmem((4, z.length, z.feats), BF16), vmem((2, z.length, z.feats), BF16), vmem(half_state, BF16),
        vmem(state, BF16), vmem(state, F32), vmem(state, BF16), vmem(slots, BF16), vmem(slots, BF16), vmem(slots, BF16),
        vmem((z.feats, seqs * z.length), BF16), vmem(half_state, BF16), vmem((4, *half_state), BF16),
        vmem(heads_state, F32), vmem(heads_state, BF16), vmem(heads_state, BF16), vmem(dqkv, BF16),
        vmem(small, F32), vmem(small, F32),
        vmem((4, z.length, z.feats), BF16), vmem((2, z.length, z.feats), BF16), vmem(half_state, BF16),
        vmem((messages, z.length - DIRECT_ROWS, z.mine), BF16),
    ] + dma(4, *[messages] * 6, 4, 4, 4, 4, 6, 6, 4, 4, 4, 4, 5, 2, 2, 8, 8, 8, 10, *[planes, planes, planes, 1] * 2, *[planes, planes, 1] * 2, 2) + [pltpu.SemaphoreType.REGULAR((2,))]
    args = (wide, x0, c0, gain_a, gain_f, cosine, sine, wqkv, wo, wu, wd)
    return call(main_kernel, "main", 1, out_shape, (0, 3, 4, 5, 6), (16, 17), scratch, args, 10**11)


def run_last(
    wide, e, dc, gain_a, gain_a_in, gain_f_in, cosine, sine, wqkv, wo, q, k, v, p, xa, ra, dqkv, every_o, every_d, every_flag, every_g, ig,
):
    seqs, length, feats = e.shape
    z = Sizes(feats, wo.shape[1], 8, length // 2)
    planes, hidden = every_g.shape[0], 8 * every_g.shape[3]
    share = feats // planes
    state, half_state, heads_state = (seqs, length, feats), (seqs, z.tokens, feats), (seqs, length, z.mine)
    messages, row, pieces = seqs + 6, (8, feats), (planes, 3, share, z.cols)
    out_shape = [
        shape(ig.shape, BF16), shape(every_g.shape, BF16), shape((3, share, z.cols), F32), shape((share, z.cols), F32),
        shape((share, hidden), F32), shape(row, F32),
    ]
    scratch = like(e, dc, wqkv, wo, q, k, v, p, xa, ra) + [
        vmem(state, BF16),
        vmem(heads_state, F32), vmem(heads_state, BF16), vmem(heads_state, BF16), vmem(dqkv.shape, BF16),
        vmem(half_state, BF16), vmem(half_state, BF16),
        vmem((6, 8, length), F32), vmem((6, 8, length), F32), vmem((2, length, feats), BF16), vmem(half_state, BF16),
        vmem((messages, length - DIRECT_ROWS, z.mine), BF16),
        vmem((feats, seqs * length), BF16), vmem((planes, share, seqs * length), BF16), vmem((3, feats, z.cols), BF16),
        vmem(pieces, BF16), vmem(pieces, BF16), vmem(every_g.shape[1:], BF16), vmem(every_o.shape[1:], BF16),
        vmem(every_d.shape[1:], BF16), vmem(every_flag.shape, F32), vmem((share, hidden), F32), vmem((share, z.cols), F32),
        vmem(row, F32), vmem(row, F32), vmem((planes, *row), F32), vmem(row, F32),
    ] + dma(12, *[messages] * 6, 4, 4, 2, 2, 2, 2, 2, planes, planes, planes, planes, planes, 1, planes, planes, 1, 1, 1, *[3 * planes] * 4, 2, 2)
    args = (wide, e, dc, gain_a, gain_a_in, gain_f_in, cosine, sine, wqkv, wo, q, k, v, p, xa, ra, dqkv, every_o, every_d, every_flag, every_g, ig)
    return call(last_kernel, "last", 3, out_shape, (0, 3, 4, 5, 6, 7), (2, 5), scratch, args, 10**8, {20: 1, 21: 0})


def local(inputs, cotangent, width_index, qkv_weight, out_weight, attn_gain, ffn_gain, up_weight, down_weight):
    seqs, tokens, width = inputs.shape
    swap = width_index[0] > width_index[1]
    flag = (jnp.max(width_index) == 3).astype(F32)
    row = lax.broadcasted_iota(jnp.int32, (8, 128), 0)
    wide = jnp.where(row == 0, flag, jnp.where(row == 1, swap.astype(F32), 0.0))

    cosine, sine = rotary(2 * tokens, HEAD_DIM)
    gain_a = attn_gain.astype(F32)[None]
    gain_f = ffn_gain.astype(F32)[None]
    layer_out, input_grad, q, k, v, p, xa, ra, every_g, every_o, every_d, every_flag, up_term, dc, e, dqkv, gain_a_term, gain_f_term = run_main(
        wide, inputs, cotangent, gain_a, gain_f, cosine, sine, qkv_weight, out_weight, up_weight, down_weight
    )
    up_sum = lax.psum_scatter(up_term.reshape(up_weight.shape), "dp", scatter_dimension=0, tiled=True)
    input_grad, _, qkv_grad, out_grad, down_grad, gains = run_last(
        wide, e, dc, gain_a, gain_a_term, gain_f_term, cosine, sine, qkv_weight, out_weight, q, k, v, p, xa, ra, dqkv,
        every_o, every_d, every_flag, every_g, input_grad,
    )
    up_sum, qkv_grad = lax.optimization_barrier((up_sum, qkv_grad))
    size = gains.shape[1] // (2 * lax.axis_size("dp"))
    own = (lax.axis_index("dp") * 2 + lax.axis_index("mp")) * size
    gain_grads = lax.dynamic_slice_in_dim(gains[:2], own, size, axis=1)
    return (
        layer_out[None],
        input_grad[None],
        qkv_grad,
        out_grad,
        gain_grads[0],
        gain_grads[1],
        up_sum.astype(F32),
        down_grad,
    )


def solution(mesh):
    in_specs = (
        P("dp", "mp", None),
        P("dp", "mp", None),
        P("dp"),
        P(None, "section", "mp"),
        P("section", "mp"),
        P("section"),
        P("section"),
        P("section", "mp"),
        P("section", "mp"),
    )
    out_specs = (
        P("section", "dp", "mp", None),
        P("section", "dp", "mp", None),
        P(None, ("section", "dp"), "mp"),
        P(("section", "dp"), "mp"),
        P(("section", "dp", "mp")),
        P(("section", "dp", "mp")),
        P(("section", "dp"), "mp"),
        P(("section", "dp"), "mp"),
    )
    return jax.shard_map(local, mesh=mesh, in_specs=in_specs, out_specs=out_specs, check_vma=False)
```

profile of v0, /device:TPU:22, one launch (start us, length us, event | category | flops | bytes accessed | tf_op | source)
XLA Modules:
  0.0 420.8 jit_solution(9618474888009186592)
XLA Ops:
  7.2 0.0 reduce-scatter.2.cloned.1.call-start
  7.2 1.3 fusion
  8.5 1.3 reduce_max.9
  11.8 1.3 reshape.24.gain_a_ref
  13.1 1.3 reshape.25.gain_f_ref
  14.3 0.7 broadcast_select_fusion.wide_ref
  15.0 222.7 %main.1 = (bf16[2,128,1536]{2,1,0:T(8,128)(2,1)}, bf16[2,128,1536]{2,1,0:T(8,128)(2,1)}, bf16[2,256,384]{2,1,0:T(8,128)(2,1)}, bf16[2,256,384]{2,1,0:T(8,128)(2,...) custom-call(f32[8,128]{1,0:T(8,128)} %broadcast_select_fusion.wide_r, ...), custom_call_target="tpu_custom_call" | custom-call | flops 99999997952 | bytes 1000000 | tf_op jit(solution)/shard_map/main/pallas_call | solution.py:1173
  237.7 0.0 reduce-scatter.2.cloned.1.call-update
  237.8 165.7 %last.1 = (bf16[2,128,1536]{2,1,0:T(8,128)(2,1)}, bf16[4,9,256,384]{3,2,1,0:T(8,128)(2,1)}, f32[3,192,768]{2,1,0:T(8,128)}, f32[192,768]{1,0:T(8,128)}, f32[192,3072]{1,0:T(8,128)}, /*index=5*/f32[8,768]{1,0:T(8,128)}) custom-call(f32[8,128]{1,0:T(8,128)} %broadcast_select_fusion.wide_ref, ...), custom_call_target="tpu_custom_call", output_to_operand_aliasing={{1}: (20, {}), {0}: (21, {})} | custom-call | flops 100000000 | bytes 1000000 | tf_op jit(solution)/shard_map/last/pallas_call | solution.py:1173
  403.5 0.0 copy-start.3
  403.5 0.8 slice.17
  404.3 0.1 constant_dynamic-slice_fusion
  404.4 0.5 slice_bitcast_fusion
  404.9 0.0 reduce-scatter.2.cloned.1.call-done
  404.9 0.0 copy-start
  404.9 3.0 convert_element_type.17
  407.9 0.0 copy-start.2
  407.9 0.0 copy-done.3
  407.9 0.9 copy.28
  408.8 0.0 copy-done
  408.8 0.0 copy-start.4
  408.8 0.9 copy.29
  409.7 0.0 copy-done.2
  409.7 0.0 copy-start.1
  409.7 1.2 copy.30
  410.9 0.0 copy-done.4
  410.9 0.8 copy.31
  411.7 0.5 copy-done.1
  412.2 1.4 copy.32
  (2 shorter events, 0.0 us)
Async XLA Ops:
  7.2 397.7 %reduce-scatter.2.cloned.1.call-start = ((), (), s32[]{:S(2)}) async-start(), calls=%async_computation.1 | async-start | bytes 5898240 | tf_op jit(solution)/shard_map/reduce_scatter | solution.py:1261
  403.5 4.4 %copy-start.3 = (bf16[2,128,1536]{2,1,0:T(8,128)(2,1)S(1)}, bf16[2,128,1536]{2,1,0:T(8,128)(2,1)}, u32[]{:S(2)}) copy-start(bf16[2,128,1536]{2,1,0:T(8,128)(2,1)} %get-tuple-element.33) | copy-start | bytes 2359300
  404.9 3.9 copy-start
  407.9 1.8 copy-start.2
  408.8 2.1 copy-start.4
  409.7 2.6 copy-start.1
Sparse Core Ops, SparseCore 0:
  237.9 158.7 reduce-scatter.1
where the time goes:
time: 426 us; the launch traced here: 421 us
  Pallas kernels  388 us (91%)
  between operations  16.3 us (4%)
  local copies, waits for them, and re-layouts  11 us (3%)
  other arithmetic  4.98 us (1%)
    pallas_call x2, Pallas kernels, call(): pl.pallas_call(kernel, out_shape=tuple(out_shape), in_specs=[IN_VMEM if n...  388 us
  transfers between devices with their start and end apart: 1, of which 0 were waited for; matrix products, arithmetic and copies ran while one was open for 0% of the time, Pallas kernels for 39%

commit v1 on v0

v1 whole, which is shorter than its diff:
```python
import functools
import types

import jax
import jax.numpy as jnp
import numpy as np
from jax import lax
from jax.sharding import PartitionSpec as P
from jax.experimental import pallas as pl
from jax.experimental.pallas import tpu as pltpu

HEAD_DIM = 128
EPSILON = 1e-05
GELU_C = 0.7978845608028654
GELU_A = 0.044715
MESH = pl.DeviceIdType.MESH
SLOTS = 10
LAG = 5
GRADS_TURN = 10
DIRECT_ROWS = 144
F32 = jnp.float32
BF16 = jnp.bfloat16
VMEM_LIMIT = 62 * 2**20


def mm(a, b):
    return lax.dot_general(a, b, (((1,), (0,)), ((), ())), preferred_element_type=F32)


def mm_nt(a, b):
    return lax.dot_general(a, b, (((1,), (1,)), ((), ())), preferred_element_type=F32)


def mm_tn(a, b):
    return lax.dot_general(a, b, (((0,), (0,)), ((), ())), preferred_element_type=F32)


def to_row(column):
    rows = column.shape[0]
    return jnp.transpose(jnp.broadcast_to(column, (rows, 128)))[:8]


def from_row(row):
    return jnp.transpose(row)[:, :1]


def rotary(length, head_size):
    half_dim = head_size // 2
    frequency = np.float32(10000.0) ** (np.float32(-2.0 / head_size) * np.arange(half_dim, dtype=np.float32))
    angles = np.arange(length, dtype=np.float32)[:, None] * frequency[None, :].astype(np.float32)
    cosine, sine = np.cos(angles).astype(np.float32), np.sin(angles).astype(np.float32)
    return jnp.asarray(np.concatenate([cosine, cosine], axis=1)), jnp.asarray(np.concatenate([-sine, sine], axis=1))


def turned(values):
    return pltpu.roll(values, HEAD_DIM // 2, 1)


def remote(src, dst, send_sem, recv_sem, device):
    return pltpu.make_async_remote_copy(
        src_ref=src, dst_ref=dst, send_sem=send_sem, recv_sem=recv_sem,
        device_id=device, device_id_type=MESH,
    )


class Place:
    def __init__(self):
        section, dp, mp = (lax.axis_index(name) for name in ("section", "dp", "mp"))
        self.block, self.half, self.core = section // 2, section % 2, mp
        other_half = 1 - self.half
        other_block = 1 - self.block
        self.at = (section, dp, mp)
        self.core_peer = (section, dp, 1 - mp)
        self.pair = (self.block * 2 + other_half, dp, mp)
        self.across = (other_block * 2 + self.half, dp, mp)
        self.corner = (other_block * 2 + other_half, dp, mp)

    def plane(self, n):
        section, dp, mp = self.at
        return (section, lax.rem(dp + n, lax.axis_size("dp")), mp)

    def barrier(self):
        sem = pltpu.get_barrier_semaphore()
        peers = [self.core_peer, self.pair, self.across, self.corner]
        peers += [self.plane(n) for n in range(1, lax.axis_size("dp"))]
        for peer in peers:
            pl.semaphore_signal(sem, inc=1, device_id=peer, device_id_type=MESH)
        pl.semaphore_wait(sem, len(peers))


class Exchange:
    def __init__(self, place, piece, slots, sems):
        self.place, self.piece, self.slots = place, piece, slots
        self.send, self.recv, self.local = sems
        self.me, self.count = lax.axis_index("dp"), lax.axis_size("dp")

    def copy(self, n):
        target = lax.rem(self.me + n, self.count)
        return remote(self.piece(target), self.slots.at[self.me], self.send.at[n], self.recv.at[n], self.place.plane(n))

    def own(self):
        return pltpu.make_async_copy(self.piece(self.me), self.slots.at[self.me], self.local.at[0])

    def start(self):
        self.own().start()
        for n in range(1, self.count):
            self.copy(n).start()

    def finish(self):
        self.own().wait()
        for n in range(1, self.count):
            source = lax.rem(self.me + self.count - n, self.count)
            held = self.slots.at[source]
            remote(held, held, self.send.at[n], self.recv.at[n], self.place.plane(n)).wait_recv()
            self.copy(n).wait_send()


class PairLink:
    def __init__(self, place, relay, sems, targets):
        self.place, self.relay, self.targets = place, relay, targets
        self.send, self.recv, self.far_send, self.far_recv, self.relay_send, self.relay_recv = sems
        rows = DIRECT_ROWS + relay.shape[1]
        self.direct = slice(0, DIRECT_ROWS)
        self.detour = slice(DIRECT_ROWS, rows)
        self.sources = {}

    def near(self, index):
        src, dst = self.sources[index](self.direct), self.targets(index, self.place.half, self.direct)
        return remote(src, dst, self.send.at[index], self.recv.at[index], self.place.pair)

    def far(self, index):
        src = self.sources[index](self.detour)
        return remote(src, self.relay.at[index], self.far_send.at[index], self.relay_recv.at[index], self.place.across)

    def whole(self, index):
        rows, src = slice(0, self.detour.stop), self.sources[index]
        dst = self.targets(index, self.place.half, rows)
        return remote(src(rows), dst, self.send.at[index], self.recv.at[index], self.place.pair)

    def start(self, index, src):
        self.sources[index] = src
        self.near(index).start()
        self.far(index).start()

    def start_near(self, index, src):
        self.sources[index] = src
        self.near(index).start()

    def start_far(self, index):
        self.far(index).start()

    def start_whole(self, index, src):
        self.sources[index] = src
        self.whole(index).start()

    def wait(self, index):
        other = 1 - self.place.half
        for rows, sem in ((self.direct, self.recv), (self.detour, self.far_recv)):
            dst = self.targets(index, other, rows)
            remote(dst, dst, self.send.at[index], sem.at[index], self.place.pair).wait_recv()

    def wait_whole(self, index):
        dst = self.targets(index, 1 - self.place.half, slice(0, self.detour.stop))
        remote(dst, dst, self.send.at[index], self.recv.at[index], self.place.pair).wait_recv()

    def finish(self, indices):
        for index in indices:
            self.near(index).wait_send()
            self.far(index).wait_send()

    def finish_whole(self, indices):
        for index in indices:
            self.whole(index).wait_send()

    def forward(self, indices):
        copies = []
        for index in indices:
            held = self.relay.at[index]
            remote(held, held, self.relay_send.at[index], self.relay_recv.at[index], self.place.across).wait_recv()
            copy = remote(held, self.targets(index, self.place.half, self.detour), self.relay_send.at[index], self.far_recv.at[index], self.place.corner)
            copy.start()
            copies.append(copy)
        for copy in copies:
            copy.wait_send()


def spread(value, width):
    return jnp.broadcast_to(value, (value.shape[0], width))


def slot_block(slot):
    return (0, slot) if slot < 2 else (1, slot - 2)


def slot_weight(slot, weight):
    unit = weight.shape[1] // 8
    at = slot_block(slot)[1] * unit
    return weight[:, at:at + unit]


def mask_slot(slot, value, flag):
    if slot == 1:
        return value * (1.0 - flag)
    return value if slot < 6 else value * flag


NARROW, WIDE = (0, 1), tuple(range(2, SLOTS))
G_PLACE = (0, 1, 2, 3, 4, 5, 9, 6, 7, 8)
DG_STRAIGHT, DG_MIDDLE, DG_LATE = (0, 1, 2), (3, 4), (5, 6, 7, 8, 9)


class Sizes:
    def __init__(self, feats, cols, hidden, tokens):
        self.feats, self.cols, self.unit, self.tokens = feats, cols, hidden // 8, tokens
        self.mine, self.length, self.width = cols // 2, 2 * tokens, 2 * feats
        self.heads = self.mine // HEAD_DIM


class Emitter:
    def __init__(self, place, out, stage, swap, sems, first=0):
        self.place, self.out, self.stage, self.swap, self.sems, self.first = place, out, stage, swap, sems, first

    def span(self):
        feats = self.stage.shape[-1]
        return pl.ds(pl.multiple_of(self.place.half * feats, feats), feats)

    def far(self, i):
        at = self.first + i
        return remote(self.stage.at[i], self.out.at[i, :, self.span()], self.sems[0].at[at], self.sems[1].at[at], self.place.pair)

    def near(self, i):
        return pltpu.make_async_copy(self.stage.at[i], self.out.at[i, :, self.span()], self.sems[2].at[self.first + i])

    def prepare(self, values):
        narrow, wide = (value.astype(F32) for value in values)
        self.stage[0] = (narrow * (1.0 - self.swap) + wide * self.swap).astype(BF16)
        self.stage[1] = (wide * (1.0 - self.swap) + narrow * self.swap).astype(BF16)

    def start(self, owner):
        @pl.when(self.place.half == owner)
        def _():
            for i in range(2):
                self.near(i).start()

        @pl.when(self.place.half != owner)
        def _():
            for i in range(2):
                self.far(i).start()

    def finish(self, owner):
        @pl.when(self.place.half == owner)
        def _():
            for i in range(2):
                self.near(i).wait()
                self.far(i).wait_recv()

        @pl.when(self.place.half != owner)
        def _():
            for i in range(2):
                self.far(i).wait_send()


class Gather:
    def __init__(self, place, mine, every, sems, first, last):
        self.me, self.count = lax.axis_index("dp"), lax.axis_size("dp")
        self.place, self.mine, self.every = place, mine, every
        self.right, self.left, self.recv, self.local = sems
        self.first, self.last = first, min(last, self.count - 1)

    def send(self, block, way, number):
        section, dp, mp = self.place.at
        sems = self.right if way > 0 else self.left
        src = self.mine if number == 1 else self.every.at[block]
        return remote(src, self.every.at[block], sems.at[block], self.recv.at[block], (section, dp + way, mp))

    def arrive(self, block):
        held = self.every.at[block]
        remote(held, held, self.right.at[block], self.recv.at[block], self.place.pair).wait_recv()

    def moves(self, number):
        me, last = self.me, self.count - 1
        right, left = me - number + 1, me + number - 1
        return ((1, right, (right >= 0) & (me < last)), (-1, left, (left <= last) & (me > 0)))

    def own(self):
        return pltpu.make_async_copy(self.mine, self.every.at[self.me], self.local.at[0])

    def step(self, number):
        if number == 1:
            self.own().start()
        if number > self.last:
            return
        for way, block, active in self.moves(number):
            @pl.when(active)
            def _(way=way, block=block):
                if number > self.first:
                    self.arrive(block)
                self.send(block, way, number).start()

    def rest(self, number):
        for more in range(number, self.last + 1):
            self.step(more)

    def finish(self):
        for number in range(self.first, self.last + 1):
            left, right = self.me - number, self.me + number
            done = number == self.last

            @pl.when((left >= 0) if done else (left >= 0) & (self.me == self.count - 1))
            def _(block=left):
                self.arrive(block)

            @pl.when((right < self.count) if done else (right < self.count) & (self.me == 0))
            def _(block=right):
                self.arrive(block)

            for way, block, active in self.moves(number):
                @pl.when(active)
                def _(way=way, block=block):
                    self.send(block, way, number).wait_send()
        if self.first == 1:
            self.own().wait()


class Scatter:
    def __init__(self, place, piece, landing, sends, arrivals, slots, intake, in_sem, chunks):
        self.place, self.piece, self.landing, self.sends, self.arrivals = place, piece, landing, sends, arrivals
        self.slots, self.intake, self.in_sem, self.chunks = slots, intake, in_sem, chunks
        self.me, self.count = lax.axis_index("dp"), lax.axis_size("dp")

    def send(self, way, target, chunk, src):
        section, dp, mp = self.place.at
        at = target * self.chunks + chunk
        return remote(src, self.landing[way].at[target, chunk], self.sends[way].at[at], self.arrivals[way].at[at], (section, dp + way, mp))

    def fetch(self, way, target, chunk):
        at = target * self.chunks + chunk
        held = self.landing[way].at[target, chunk]
        remote(held, held, self.sends[way].at[at], self.arrivals[way].at[at], self.place.pair).wait_recv()
        copy = pltpu.make_async_copy(held, self.intake[way], self.in_sem.at[0])
        copy.start()
        copy.wait()
        return self.intake[way][...].astype(F32)

    def each(self, way, body):
        def step_body(step, carry):
            body(step, self.count - 1 - step if way > 0 else step)
            return carry
        lax.fori_loop(0, self.count - 1, step_body, 0)

    def from_edge(self, way, chunk):
        @pl.when(self.me == (0 if way > 0 else self.count - 1))
        def _():
            self.each(way, lambda step, target: self.send(way, target, chunk, self.piece(chunk, target)).start())

    def edges(self, chunk):
        self.from_edge(1, chunk)
        self.from_edge(-1, chunk)

    def between(self, way, target):
        if way > 0:
            return (self.me > 0) & (self.me < target)
        return (self.me < self.count - 1) & (self.me > target)

    def turns(self):
        return range(self.chunks + max(self.count - 3, 0))

    def middle(self, turn):
        if self.count < 3 or turn not in self.turns():
            return
        def pass_on(way, step, target):
            depth = self.me if way > 0 else self.count - 1 - self.me
            chunk = turn + 1 - depth

            @pl.when(self.between(way, target) & (chunk >= 0) & (chunk < self.chunks))
            def _():
                slot = self.slots(way, lax.rem(chunk, 2) * (self.count - 1) + step)
                total = self.fetch(way, target, chunk) + self.piece(chunk, target)[...].astype(F32)

                @pl.when(chunk >= 2)
                def _():
                    self.send(way, target, chunk - 2, slot).wait_send()

                slot[...] = total.astype(BF16)
                self.send(way, target, chunk, slot).start()

        def both(step, carry):
            pass_on(1, step, self.count - 1 - step)
            pass_on(-1, step, step)
            return carry

        lax.fori_loop(0, self.count - 1, both, 0)

    def last(self, chunk, total_ref):
        total_ref[...] = self.piece(chunk, self.me)[...].astype(F32)
        for way, there in ((1, self.me > 0), (-1, self.me < self.count - 1)):
            @pl.when(there)
            def _(way=way):
                total_ref[...] = total_ref[...] + self.fetch(way, self.me, chunk)

    def finish(self):
        for way in (1, -1):
            edge = self.me == (0 if way > 0 else self.count - 1)

            def sent(chunk, step, target, way=way, edge=edge):
                active = (edge | self.between(way, target)) if chunk >= self.chunks - 2 else edge

                @pl.when(active)
                def _():
                    self.send(way, target, chunk, self.piece(chunk, target)).wait_send()

            for chunk in range(self.chunks):
                self.each(way, functools.partial(sent, chunk))


def main_kernel(names, *refs):
    r = types.SimpleNamespace(**dict(zip(names, refs)))
    place = Place()
    half, core = place.half, place.core
    me, planes = lax.axis_index("dp"), lax.axis_size("dp")
    seqs, length, feats = r.xa.shape
    z = Sizes(feats, r.wo.shape[1], r.wud.shape[2], length // 2)
    mine, unit = z.mine, z.unit
    share = feats // planes

    r.wu, r.wd = r.wud.at[0], r.wud.at[1]
    weights = ((r.wqkv_hbm, r.wqkv), (r.wo_hbm, r.wo), (r.wu_hbm, r.wu), (r.wd_hbm, r.wd))

    @pl.when(place.block == 0)
    def _():
        for n in range(4):
            pltpu.make_async_copy(*weights[n], r.load_sem.at[n]).start()

    @pl.when(place.block == 1)
    def _():
        for n in range(3, -1, -1):
            pltpu.make_async_copy(*weights[n], r.load_sem.at[n]).start()

    def loaded(n):
        pltpu.make_async_copy(*weights[n], r.load_sem.at[n]).wait()

    first_width, second_width = r.width[0], r.width[1]
    r.wide[...] = jnp.zeros_like(r.wide)
    r.wide[0:1, :] = jnp.full((1, 128), 1.0 - 0.5 * (first_width * second_width).astype(F32), F32)
    r.wide[1:2, :] = jnp.full((1, 128), lax.shift_right_logical(first_width, 1).astype(F32), F32)
    flag, swap = r.wide[0:1, :1], r.wide[1:2, :1]
    gain_a = r.gain_a[...].reshape(1, feats).astype(F32)
    gain_f = r.gain_f[...].reshape(1, feats).astype(F32)

    place.barrier()

    first_u, first_dg = 6 + seqs, 6 + seqs + SLOTS
    first_do = first_dg + SLOTS
    first_dqkv = first_do + seqs

    def targets(index, sender_half, rows):
        span = pl.ds(pl.multiple_of(sender_half * mine, mine), mine)
        if index < 6:
            return r.rcv_qkv.at[index // 3, index % 3, rows, :]
        if index < first_u:
            return r.o.at[index - 6, rows, span]
        if index < first_dg:
            return r.rcv_u.at[index - first_u, rows, :]
        if index < first_do:
            return r.rcv_dg.at[index - first_dg, rows, :]
        if index < first_dqkv:
            return r.rcv_do.at[index - first_do, rows, :]
        n = index - first_dqkv
        return r.dqkv.at[n // 3, n % 3, rows, span]

    link = PairLink(place, r.relay, (r.x_send, r.x_recv, r.far_send, r.far_recv, r.relay_send, r.relay_recv), targets)
    forward_order = tuple(range(first_dg))
    ffn_order = tuple(range(first_dg, first_do))
    do_order = tuple(range(first_do, first_dqkv))
    dqkv_order = tuple(range(first_dqkv, first_dqkv + 6))
    my_rows = pl.ds(pl.multiple_of(core * z.tokens, z.tokens), z.tokens)
    their_rows = pl.ds(pl.multiple_of((1 - core) * z.tokens, z.tokens), z.tokens)
    my_feats = pl.ds(pl.multiple_of(half * feats, feats), feats)

    def share_rows(n):
        return pl.ds(pl.multiple_of(n * share, share), share)

    gather = Gather(place, r.g.at[0:SLOTS - 1], r.every_g, (r.g_right, r.g_left, r.g_sem, r.g_local), 1, length)
    gather_o = Gather(place, r.o, r.every_o, (r.o_right, r.o_left, r.o_sem, r.o_local), 1, length)
    exchange_d = Exchange(place, lambda n: r.dt.at[share_rows(n), :], r.every_d, (r.d_send, r.d_recv, r.d_local))
    exchange_c = Exchange(place, lambda n: r.dt.at[share_rows(n), :], r.every_c, (r.c_send, r.c_recv, r.c_local))
    exchange_flag = Exchange(place, lambda n: r.wide, r.every_flag, (r.flag_send, r.flag_recv, r.flag_local))
    exchange_flag.start()

    def local_copy(src, dst, n):
        return pltpu.make_async_copy(src, dst, r.in_local.at[n])

    def core_half(src, dst, n):
        return remote(src, dst, r.in_send.at[n], r.in_recv.at[n], place.core_peer)

    def x_copy(i):
        return remote(r.x2.at[i], r.xa.at[i, my_rows, :], r.y_send.at[i], r.y_recv.at[i], place.across)

    def e_copy(i):
        return remote(r.e_out.at[i], r.e_in.at[i, my_rows, :], r.y_send.at[i], r.y_recv.at[i], place.across)

    def start_half(src_ref, dst_ref, first):
        for i in range(seqs):
            local_copy(src_ref.at[i, :, my_feats], dst_ref.at[i, my_rows, :], first + i).start()
            core_half(src_ref.at[i, :, my_feats], dst_ref.at[i, my_rows, :], first + i).start()

    def ordered_halves(raw_ref, dst_ref, first):
        for i in range(seqs):
            local_copy(raw_ref.at[i, my_rows, :], raw_ref.at[i, my_rows, :], first + i).wait()
            core_half(raw_ref.at[i, my_rows, :], raw_ref.at[i, my_rows, :], first + i).wait()
        for i in range(seqs):
            mixed = raw_ref[i].astype(F32) * (1.0 - swap) + raw_ref[1 - i].astype(F32) * swap
            dst_ref[i] = mixed.astype(BF16)

    def pass_half(dst_ref, n, i):
        core_half(dst_ref.at[i, my_rows, :], dst_ref.at[i, my_rows, :], n).start()
        core_half(dst_ref.at[i, my_rows, :], dst_ref.at[i, my_rows, :], n).wait()

    def sq_copy(n):
        return remote(r.snd_sq.at[n], r.rcv_sq.at[n], r.sq_send.at[n], r.sq_recv.at[n], place.pair)

    def core_copy(n):
        return remote(r.snd_br.at[n], r.rcv_br.at[n], r.core_send.at[n], r.core_recv.at[n], place.core_peer)

    def core_rows(i):
        return remote(r.snd_br.at[2 + i, their_rows, :], r.rcv_half.at[i], r.core_send.at[2 + i], r.core_recv.at[2 + i], place.core_peer)

    def row_copy(n, peer):
        return remote(r.snd_row.at[n], r.rcv_row.at[n], r.row_send.at[n], r.row_recv.at[n], peer)

    def db_copy(n):
        return remote(r.snd_db.at[n], r.rcv_db.at[n], r.db_send.at[n], r.db_recv.at[n], place.core_peer)

    def da_rows(i):
        return remote(r.snd_db.at[2 + i, their_rows, :], r.rcv_da.at[i], r.db_send.at[2 + i], r.db_recv.at[2 + i], place.core_peer)

    def ready(n):
        pl.semaphore_signal(r.go_sem.at[n], inc=1, device_id=place.pair, device_id_type=MESH)

    def wait_ready(n):
        pl.semaphore_wait(r.go_sem.at[n], 1)

    out_sems = (r.out_send, r.out_recv, r.out_local)
    emit_x1 = Emitter(place, r.layer_out, r.stage.at[0], swap, out_sems, 0)
    emit_x2 = Emitter(place, r.layer_out, r.stage.at[1], swap, out_sems, 2)
    emit_e1 = Emitter(place, r.input_grad, r.stage.at[2], swap, out_sems, 4)
    emit_e0 = Emitter(place, r.input_grad, r.stage.at[3], swap, out_sems, 6)
    theirs = pl.multiple_of((1 - half) * mine, mine)
    ours = pl.multiple_of(half * mine, mine)

    def dg_part(slot):
        r.snd_dg[slot] = mm(r.e_in[slot_block(slot)[0]], slot_weight(slot, r.wd)).astype(BF16)

    def dg_source(slot):
        return lambda rows: r.snd_dg.at[slot, rows, :]

    def transposed(src_ref):
        for i in range(seqs):
            r.dt[:, i * length:(i + 1) * length] = jnp.transpose(src_ref[i].astype(F32)).astype(BF16)

    @pl.when(place.block == 0)
    def _():
        start_half(r.x0, r.xf, 0)
        ordered_halves(r.xf, r.xa, 0)

    @pl.when(place.block == 1)
    def _():
        start_half(r.c0, r.dc, 2)
        loaded(3)
        ordered_halves(r.dc, r.e_in, 2)
        for slot in range(SLOTS):
            dg_part(slot)
        transposed(r.e_in)
        exchange_d.start()
        link.forward(forward_order[:6])
        link.start_whole(first_dg, dg_source(0))
        link.forward(forward_order[6:8])
        link.start_whole(first_dg + 1, dg_source(1))
        link.forward(forward_order[8:])
        link.start_whole(first_dg + 2, dg_source(2))

    for i in range(seqs):
        @pl.when(place.block == 1)
        def _():
            x_copy(i).wait_recv()
            if i == 1:
                ready(0)
            pass_half(r.xa, i, i)

        x = r.xa[i].astype(F32)
        r.snd_sq[i] = to_row(jnp.sum(x * x, axis=-1, keepdims=True))
        sq_copy(i).start()
        r.xg[i] = (x * gain_a).astype(BF16)
        if i == 0:
            loaded(0)
        for t in range(3):
            r.snd_qkv[i, t] = mm(r.xg[i], r.wqkv[t, :, pl.ds(theirs, mine)]).astype(BF16)
            source = lambda rows, i=i, t=t: r.snd_qkv.at[i, t, rows, :]

            @pl.when(place.block == 0)
            def _():
                link.start(3 * i + t, source)

            @pl.when(place.block == 1)
            def _():
                if i == 0:
                    link.start_whole(t, source)
                else:
                    link.start_near(3 + t, source)

    @pl.when(place.block == 1)
    def _():
        wait_ready(0)
        for t in range(3):
            link.start_far(3 + t)

    for i in range(seqs):
        for t in range(3):
            r.own_qkv[i, t] = mm(r.xg[i], r.wqkv[t, :, pl.ds(ours, mine)])

    cosine, sine = r.cosine[...], r.sine[...]
    scale = HEAD_DIM ** (-0.5)
    causal = lax.broadcasted_iota(jnp.int32, (length, length), 0) >= lax.broadcasted_iota(jnp.int32, (length, length), 1)
    for i in range(seqs):
        sq_copy(i).wait_recv()
        factor = lax.rsqrt((from_row(r.snd_sq[i]) + from_row(r.rcv_sq[i])) * (1.0 / z.width) + EPSILON)
        r.ra[i] = spread(factor, 128)
        if i == 0:
            @pl.when(place.block == 0)
            def _():
                for t in range(3):
                    link.wait(t)

            @pl.when(place.block == 1)
            def _():
                for t in range(3):
                    link.wait_whole(t)
        else:
            for t in range(3):
                link.wait(3 + t)
        for j in range(z.heads):
            span = pl.ds(j * HEAD_DIM, HEAD_DIM)
            raw = [(r.own_qkv[i, t, :, span] + r.rcv_qkv[i, t, :, span].astype(F32)) * factor for t in range(3)]
            q_j = (raw[0] * cosine + turned(raw[0]) * sine).astype(BF16)
            k_j = (raw[1] * cosine + turned(raw[1]) * sine).astype(BF16)
            v_j = raw[2].astype(BF16)
            r.q[i, :, span], r.k[i, :, span], r.v[i, :, span] = q_j, k_j, v_j
            scores = jnp.where(causal, mm_nt(q_j, k_j) * scale, -1e30)
            exponent = jnp.exp(scores - jnp.max(scores, axis=-1, keepdims=True))
            probs = exponent / jnp.sum(exponent, axis=-1, keepdims=True)
            r.p[i, j] = probs
            r.o[i, :, pl.ds(pl.multiple_of(ours + j * HEAD_DIM, HEAD_DIM), HEAD_DIM)] = mm(probs.astype(BF16), v_j).astype(BF16)
        link.start(6 + i, lambda rows, i=i: r.o.at[i, rows, pl.ds(ours, mine)])

    loaded(1)
    for i in range(seqs):
        link.wait(6 + i)
        r.snd_br[i] = mm_nt(r.o[i], r.wo[...]).astype(BF16)
        core_copy(i).start()

    @pl.when(place.block == 1)
    def _():
        for slot in DG_MIDDLE:
            link.start(first_dg + slot, dg_source(slot))

    gather_o.step(1)

    def slot_start(slot):
        part = mm(r.xg[slot_block(slot)[0]], slot_weight(slot, r.wu))
        r.u[slot] = part
        r.snd_u[slot] = part.astype(BF16)
        link.start(first_u + slot, lambda rows: r.snd_u.at[slot, rows, :])

    loaded(2)
    for i, slots in enumerate((NARROW, WIDE)):
        core_copy(i).wait_recv()
        r.xf[i] = (r.xa[i].astype(F32) + (r.snd_br[i].astype(F32) + r.rcv_br[i].astype(F32))).astype(BF16)
        x = r.xf[i].astype(F32)
        r.snd_sq[2 + i] = to_row(jnp.sum(x * x, axis=-1, keepdims=True))
        sq_copy(2 + i).start()
        r.xg[i] = (x * gain_f).astype(BF16)
        for slot in slots:
            slot_start(slot)

    @pl.when(place.block == 1)
    def _():
        for slot in DG_LATE:
            link.start(first_dg + slot, dg_source(slot))

    emit_x1.prepare([r.xf[i, my_rows, :] for i in range(seqs)])
    factors = {}

    def row_factor(i):
        sq_copy(2 + i).wait_recv()
        factors[i] = lax.rsqrt((from_row(r.snd_sq[2 + i]) + from_row(r.rcv_sq[2 + i])) * (1.0 / z.width) + EPSILON)
        r.rf[i] = spread(factors[i], 128)

    def activate(slot):
        link.wait(first_u + slot)
        value = (r.u[slot] + r.rcv_u[slot].astype(F32)) * factors[slot_block(slot)[0]]
        squared = value * value
        bent = jnp.tanh(GELU_C * (value + GELU_A * (squared * value)))
        slope = 0.5 * (1.0 + bent) + 0.5 * value * (1.0 - bent * bent) * (GELU_C * (1.0 + 3.0 * GELU_A * squared))
        r.u[slot] = value
        r.rcv_u[slot] = mask_slot(slot, slope, flag).astype(BF16)
        g_k = mask_slot(slot, 0.5 * value * (1.0 + bent), flag).astype(BF16)
        r.g[G_PLACE[slot]] = g_k
        return mm_nt(g_k, slot_weight(slot, r.wd))

    def finish_rows(i):
        core_rows(i).wait_recv()
        total = r.snd_br[2 + i, my_rows, :].astype(F32) + r.rcv_half[i].astype(F32)
        r.x2[i] = (r.xf[i, my_rows, :].astype(F32) + total).astype(BF16)

        @pl.when(place.block == 0)
        def _():
            x_copy(i).start()

    @pl.when(place.block == 0)
    def _():
        loaded(3)

    row_factor(0)
    r.snd_br[2] = (activate(0) + activate(1)).astype(BF16)
    core_rows(0).start()
    gather_o.step(2)
    row_factor(1)
    total = activate(2) + activate(3)
    finish_rows(0)
    for slot in WIDE[2:]:
        total = total + activate(slot)
    r.snd_br[3] = total.astype(BF16)
    core_rows(1).start()
    r.g[1] = r.g[1] + r.g[SLOTS - 1]
    finish_rows(1)
    emit_x2.prepare([r.x2[i] for i in range(seqs)])
    gather.step(1)
    gather_o.rest(3)

    def piece(chunk, target):
        column = pl.multiple_of(lax.rem(chunk, 8) * unit, unit)
        return r.wud.at[lax.div(chunk, 8), share_rows(target), pl.ds(column, unit)]

    def slots(way, n):
        per = max(length // share, 1)
        ref = r.snd_qkv if way > 0 else r.rcv_qkv
        at = lax.div(n, per)
        return ref.at[lax.div(at, 3), lax.rem(at, 3), share_rows(lax.rem(n, per)), :]

    intake = {1: r.snd_u.at[0, 0:share, :], -1: r.snd_u.at[1, 0:share, :]}
    scatter = Scatter(
        place, piece, {1: r.from_left, -1: r.from_right}, {1: r.sum_right, -1: r.sum_left}, {1: r.got_left, -1: r.got_right},
        slots, intake, r.intake_sem, 14,
    )

    @pl.when(place.block == 0)
    def _():
        link.forward(forward_order[3:first_u])
        link.forward(tuple(first_dg + slot for slot in DG_MIDDLE))
        link.forward(forward_order[first_u:])
        gather.step(2)
        link.forward(tuple(first_dg + slot for slot in DG_LATE))
        link.forward(do_order + dqkv_order)
        gather.rest(3)
        for i, slot_list in enumerate((NARROW, WIDE)):
            e_copy(i).wait_recv()
            if i == 1:
                ready(1)
            pass_half(r.e_in, 2 + i, i)
            for slot in slot_list:
                dg_part(slot)
                if i == 0:
                    link.start_whole(first_dg + slot, dg_source(slot))
                else:
                    link.start_near(first_dg + slot, dg_source(slot))
                if i == 1 and slot == WIDE[1]:
                    wait_ready(1)
                    for sent in WIDE[:2]:
                        link.start_far(first_dg + sent)
                if i == 1 and slot > WIDE[1]:
                    link.start_far(first_dg + slot)
        transposed(r.e_in)
        exchange_d.start()
        link.finish(forward_order[:3])

    @pl.when(place.block == 1)
    def _():
        link.finish_whole(forward_order[:3])

    link.finish(forward_order[3:])
    for i in range(seqs):
        r.xg[i] = (r.xf[i].astype(F32) * r.rf[i][:, :1] * gain_f).astype(BF16)

    def hidden_back(slot):
        @pl.when(place.block == 0)
        def _():
            (link.wait_whole if slot in NARROW else link.wait)(first_dg + slot)

        @pl.when(place.block == 1)
        def _():
            (link.wait_whole if slot in DG_STRAIGHT else link.wait)(first_dg + slot)

        grad = r.snd_dg[slot].astype(F32) + r.rcv_dg[slot].astype(F32)
        du_k = (grad * r.rcv_u[slot].astype(F32)).astype(BF16)
        r.du[slot] = du_k
        return mm_nt(du_k, slot_weight(slot, r.wu)), jnp.sum(du_k.astype(F32) * r.u[slot], axis=-1, keepdims=True)

    def up_grad(block):
        part = mm_tn(r.xg[1], r.du[2 + block])
        if block < 2:
            part = part + mm_tn(r.xg[0], r.du[block])
        r.wu[:, block * unit:(block + 1) * unit] = part.astype(BF16)
        scatter.edges(block)

    def core_sum_start(i, slot_list):
        total = row = None
        for slot in slot_list:
            more, more_row = hidden_back(slot)
            total, row = (more, more_row) if total is None else (total + more, row + more_row)

            if i == 1:
                @pl.when(place.block == 0)
                def _(slot=slot):
                    up_grad(slot - 2)

        r.snd_db[i] = total.astype(BF16)
        db_copy(i).start()
        r.snd_row[i] = to_row(row)
        row_copy(i, place.core_peer).start()

    def ffn_done(i):
        db_copy(i).wait_recv()
        row_copy(i, place.core_peer).wait_recv()
        mean = (from_row(r.snd_row[i]) + from_row(r.rcv_row[i])) * (1.0 / z.width)
        grad = r.snd_db[i].astype(F32) + r.rcv_db[i].astype(F32)
        factor = r.rf[i][:, :1]
        scaled = r.xf[i].astype(F32) * factor
        new = r.e_in[i].astype(F32) + factor * (grad * gain_f - scaled * mean)
        r.e[i] = new
        r.dc[i] = new.astype(BF16)
        r.snd_do[i] = mm(r.dc[i], r.wo[:, pl.ds(theirs, mine)]).astype(BF16)
        link.start(first_do + i, lambda rows: r.snd_do.at[i, rows, :])
        r.own_do[i] = mm(r.dc[i], r.wo[:, pl.ds(ours, mine)])
        return jnp.sum(grad * scaled, axis=0, keepdims=True)

    core_sum_start(0, NARROW)
    gain_f_sum = ffn_done(0)
    core_sum_start(1, WIDE)
    gain_f_sum = gain_f_sum + ffn_done(1)
    r.gains[...] = jnp.zeros_like(r.gains)
    r.gains[1:2, :] = 0.5 * gain_f_sum
    emit_e1.prepare([r.dc[i, my_rows, :] for i in range(seqs)])
    exchange_d.finish()
    transposed(r.dc)
    exchange_c.start()

    for i in range(seqs):
        link.wait(first_do + i)
        row = jnp.zeros((length, 1), F32)
        for j in range(z.heads):
            span = pl.ds(j * HEAD_DIM, HEAD_DIM)
            do_j = (r.own_do[i, :, span] + r.rcv_do[i, :, span].astype(F32)).astype(BF16)
            q_j, k_j, v_j, probs = r.q[i, :, span], r.k[i, :, span], r.v[i, :, span], r.p[i, j]
            dp = mm_nt(do_j, v_j)
            dv = mm_tn(probs.astype(BF16), do_j)
            ds = (probs * (dp - jnp.sum(probs * dp, axis=-1, keepdims=True))).astype(BF16)
            dq = mm(ds, k_j) * scale
            dk = mm_tn(ds, q_j) * scale
            row = row + jnp.sum(dq * q_j.astype(F32) + dk * k_j.astype(F32) + dv * v_j.astype(F32), axis=-1, keepdims=True)
            at = pl.ds(pl.multiple_of(ours + j * HEAD_DIM, HEAD_DIM), HEAD_DIM)
            r.dqkv[i, 0, :, at] = (dq * cosine - turned(dq) * sine).astype(BF16)
            r.dqkv[i, 1, :, at] = (dk * cosine - turned(dk) * sine).astype(BF16)
            r.dqkv[i, 2, :, at] = dv.astype(BF16)
        r.snd_row[2 + i] = to_row(row)
        row_copy(2 + i, place.pair).start()
        for t in range(3):
            link.start(first_dqkv + 3 * i + t, lambda rows, i=i, t=t: r.dqkv.at[i, t, rows, pl.ds(ours, mine)])
        if i == 0:
            @pl.when(place.block == 0)
            def _():
                scatter.middle(0)

    @pl.when(place.block == 0)
    def _():
        for chunk in range(1, 4):
            scatter.middle(chunk)

    for i in range(seqs):
        part = jnp.zeros((length, feats), F32)
        for t in range(3):
            link.wait(first_dqkv + 3 * i + t)
            part = part + mm_nt(r.dqkv[i, t], r.wqkv[t])
        r.snd_db[2 + i] = part.astype(BF16)
        da_rows(i).start()
        row_copy(2 + i, place.pair).wait_recv()
        r.snd_row[4 + i] = r.snd_row[2 + i] + r.rcv_row[2 + i]
        row_copy(4 + i, place.core_peer).start()

    gain_a_sum = jnp.zeros((1, feats), F32)
    for i in range(seqs):
        da_rows(i).wait_recv()
        row_copy(4 + i, place.core_peer).wait_recv()
        r.snd_row[6 + i] = (r.snd_row[4 + i] + r.rcv_row[4 + i]) * (1.0 / z.width)
        mean = from_row(r.snd_row[6 + i, :, my_rows])
        grad = r.snd_db[2 + i, my_rows, :].astype(F32) + r.rcv_da[i].astype(F32)
        factor = r.ra[i, my_rows, :][:, :1]
        scaled = r.xa[i, my_rows, :].astype(F32) * factor
        r.e_out[i] = (r.e[i, my_rows, :] + factor * (grad * gain_a - scaled * mean)).astype(BF16)
        gain_a_sum = gain_a_sum + jnp.sum(grad * scaled, axis=0, keepdims=True)

        @pl.when(place.block == 1)
        def _():
            e_copy(i).start()

    r.gains[0:1, :] = gain_a_sum
    emit_e0.prepare([r.e_out[i] for i in range(seqs)])

    def qkv_grad():
        for i in range(seqs):
            r.xg[i] = (r.xa[i].astype(F32) * r.ra[i][:, :1] * gain_a).astype(BF16)
        for t in range(3):
            r.wd[:, t * z.cols:(t + 1) * z.cols] = (mm_tn(r.xg[0], r.dqkv[0, t]) + mm_tn(r.xg[1], r.dqkv[1, t])).astype(BF16)
            for chunk in range(8 + 2 * t, 10 + 2 * t):
                scatter.edges(chunk)

    @pl.when(place.block == 1)
    def _():
        gather.step(2)
        for block in range(8):
            up_grad(block)
        qkv_grad()
        link.forward(ffn_order[len(NARROW):])
        link.forward(do_order)
        gather.rest(3)
        scatter.middle(0)
        link.forward(dqkv_order)
        for chunk in range(1, 4):
            scatter.middle(chunk)

    @pl.when(place.block == 0)
    def _():
        qkv_grad()

    emit_x1.start(0)
    emit_x2.start(1)
    emit_e1.start(1)
    emit_e0.start(0)
    gains_copy = remote(r.gains, r.core_gains, r.pair_send.at[0], r.pair_recv.at[0], place.core_peer)
    gains_copy.start()
    exchange_flag.finish()
    scatter.middle(4)
    gains_copy.wait()
    r.every_gain[me] = r.gains[...] + r.core_gains[...]
    exchange_gain = Exchange(place, lambda n: r.every_gain.at[me], r.every_gain, (r.gain_send, r.gain_recv, None))
    for n in range(1, planes):
        exchange_gain.copy(n).start()

    rows = slice(0, share)
    for n in range(SLOTS):
        r.u[n, rows, :] = jnp.zeros_like(r.u[n, rows, :])
    flags_copy = pltpu.make_async_copy(r.every_flag, r.flags, r.block_sem.at[0])
    flags_copy.start()
    flags_copy.wait()

    def plane_grads(n, carry):
        block_g = r.du.at[0:SLOTS - 1]
        sources = ((r.every_g, block_g), (r.every_o, r.xf), (r.every_d, r.block_d), (r.every_c, r.block_c))
        copies = [pltpu.make_async_copy(src.at[n], dst, r.block_sem.at[at]) for at, (src, dst) in enumerate(sources)]
        for copy in copies:
            copy.start()
        for copy in copies:
            copy.wait()
        on = r.flags[n][:1, :1]
        shared = block_g[1].astype(F32)
        upper, lower = (shared * on).astype(BF16), (shared * (1.0 - on)).astype(BF16)
        narrow, wide = r.block_d[:, :length], r.block_d[:, length:]
        for block in range(8):
            right = upper if block == 4 else block_g[2 + block if block < 4 else 1 + block]
            part = mm(wide, right)
            if block < 2:
                part = part + mm(narrow, block_g[0] if block == 0 else lower)
            r.u[block, rows, :] = r.u[block, rows, :] + part
        for side in range(2):
            span = slice(side * unit, (side + 1) * unit)
            part = mm(r.block_c[:, :length], r.xf[0, :, span]) + mm(r.block_c[:, length:], r.xf[1, :, span])
            r.u[8 + side, rows, :] = r.u[8 + side, rows, :] + part
        return carry

    def grad_copy(n):
        dst = r.down_grad.at[:, n * unit:(n + 1) * unit] if n < 8 else r.out_grad.at[:, (n - 8) * unit:(n - 7) * unit]
        return pltpu.make_async_copy(r.u.at[n, rows, :], dst, r.grad_sem.at[n])

    def total_slot(chunk):
        at = chunk % 6
        return r.own_qkv.at[at // 3, at % 3, rows, :]

    def total_copy(chunk):
        if chunk < 8:
            dst = r.up_grad.at[:, chunk * unit:(chunk + 1) * unit]
        else:
            t, side = (chunk - 8) // 2, (chunk - 8) % 2
            dst = r.qkv_grad.at[t, :, side * unit:(side + 1) * unit]
        return pltpu.make_async_copy(total_slot(chunk), dst, r.total_sem.at[chunk % 6])

    def final(chunk):
        if chunk >= 6:
            total_copy(chunk - 6).wait()
        scatter.last(chunk, total_slot(chunk))
        total_copy(chunk).start()

    for turn in range(5, 14 + LAG):
        scatter.middle(turn)
        if turn >= LAG:
            final(turn - LAG)
        if turn == GRADS_TURN:
            gather.finish()
            gather_o.finish()
            exchange_c.finish()
            lax.fori_loop(0, planes, plane_grads, 0)
            for n in range(SLOTS):
                grad_copy(n).start()
    for turn in range(14 + LAG, len(scatter.turns())):
        scatter.middle(turn)
    for n in range(1, planes):
        source = lax.rem(me + planes - n, planes)
        slot = r.every_gain.at[source]
        remote(slot, slot, r.gain_send.at[n], r.gain_recv.at[n], place.pair).wait_recv()
        exchange_gain.copy(n).wait_send()
    gain_total = r.every_gain[0]
    for n in range(1, planes):
        gain_total = gain_total + r.every_gain[n]
    r.gain_grads[...] = gain_total

    scatter.finish()
    for chunk in range(8, 14):
        total_copy(chunk).wait()
    for n in range(SLOTS):
        grad_copy(n).wait()
    for n in range(4):
        sq_copy(n).wait_send()
    for i in range(seqs):
        core_copy(i).wait_send()
        core_rows(i).wait_send()
        row_copy(i, place.core_peer).wait_send()
        row_copy(2 + i, place.pair).wait_send()
        row_copy(4 + i, place.core_peer).wait_send()
        db_copy(i).wait_send()
        da_rows(i).wait_send()
    link.finish(do_order + dqkv_order)

    @pl.when(place.block == 0)
    def _():
        link.finish_whole(ffn_order[:len(NARROW)])
        link.finish(ffn_order[len(NARROW):])
        for i in range(seqs):
            x_copy(i).wait_send()

    @pl.when(place.block == 1)
    def _():
        link.finish_whole(tuple(first_dg + slot for slot in DG_STRAIGHT))
        link.finish(tuple(first_dg + slot for slot in DG_MIDDLE + DG_LATE))
        for i in range(seqs):
            e_copy(i).wait_send()

    emit_x1.finish(0)
    emit_x2.finish(1)
    emit_e1.finish(1)
    emit_e0.finish(0)


def shape(dims, kind):
    return jax.ShapeDtypeStruct(dims, kind)


ANY = pl.BlockSpec(memory_space=pl.ANY)
IN_VMEM = pl.BlockSpec(memory_space=pltpu.VMEM)


def vmem(dims, kind):
    return pltpu.VMEM(tuple(dims), kind)


def run_main(width_index, x0, c0, gain_a, gain_f, wqkv, wo, wu, wd):
    seqs, tokens, width = x0.shape
    planes = lax.axis_size("dp")
    z = Sizes(wo.shape[0], wo.shape[1], wu.shape[1], tokens)
    share, chunks = z.feats // planes, 14
    cosine, sine = rotary(z.length, HEAD_DIM)
    args = {
        "width": width_index, "x0": x0, "c0": c0, "gain_a": gain_a, "gain_f": gain_f, "cosine": cosine, "sine": sine,
        "wqkv_hbm": wqkv, "wo_hbm": wo, "wu_hbm": wu, "wd_hbm": wd,
    }
    places = {"width": pl.BlockSpec(memory_space=pltpu.SMEM)}
    places.update({name: IN_VMEM for name in ("gain_a", "gain_f", "cosine", "sine", "gain_grads")})
    row = (8, z.feats)
    outs = {
        "layer_out": shape((seqs, tokens, width), BF16), "input_grad": shape((seqs, tokens, width), BF16),
        "qkv_grad": shape((3, share, z.cols), F32), "out_grad": shape((share, z.cols), F32),
        "up_grad": shape((share, 8 * z.unit), F32), "down_grad": shape((share, 8 * z.unit), F32), "gain_grads": shape(row, F32),
        "every_g": shape((planes, SLOTS - 1, z.length, z.unit), BF16), "every_o": shape((planes, seqs, z.length, z.cols), BF16),
        "every_d": shape((planes, share, seqs * z.length), BF16), "every_c": shape((planes, share, seqs * z.length), BF16),
        "every_flag": shape((planes, 8, 128), F32),
        "from_left": shape((planes, chunks, share, z.unit), BF16), "from_right": shape((planes, chunks, share, z.unit), BF16),
    }
    state, half_state, heads_state = (seqs, z.length, z.feats), (seqs, tokens, z.feats), (seqs, z.length, z.mine)
    slots, qkv, messages = (SLOTS, z.length, z.unit), (seqs, 3, z.length, z.mine), 12 + 2 * seqs + 2 * SLOTS
    small, factor, pair = (8, 8, z.length), (seqs, z.length, 128), (4, z.length, z.feats)
    scratch = {"wqkv": vmem(wqkv.shape, BF16), "wo": vmem(wo.shape, BF16), "wud": vmem((2, *wu.shape), BF16)}
    for dims, kind, group in (
        (state, BF16, "xa xf xg e_in dc"), (state, F32, "e"), (half_state, BF16, "x2 e_out rcv_half rcv_da"),
        (heads_state, BF16, "q k v snd_do rcv_do"), (heads_state, F32, "own_do"),
        ((seqs, z.heads, z.length, z.length), F32, "p"), ((seqs, z.length, z.cols), BF16, "o"), (factor, F32, "ra rf"),
        (slots, F32, "u"), (slots, BF16, "g snd_u rcv_u du snd_dg rcv_dg"), (qkv, F32, "own_qkv"), (qkv, BF16, "snd_qkv rcv_qkv"),
        ((4, 8, z.length), F32, "snd_sq rcv_sq"), (small, F32, "snd_row rcv_row"), (pair, BF16, "snd_br snd_db"),
        ((2, z.length, z.feats), BF16, "rcv_br rcv_db"), ((z.feats, seqs * z.length), BF16, "dt"), ((4, *half_state), BF16, "stage"),
        ((seqs, 3, z.length, z.cols), BF16, "dqkv"), ((messages, z.length - DIRECT_ROWS, z.mine), BF16, "relay"),
        ((8, 128), F32, "wide"), ((planes, 8, 128), F32, "flags"), ((share, seqs * z.length), BF16, "block_d block_c"),
        (row, F32, "gains core_gains"), ((planes, *row), F32, "every_gain"),
    ):
        scratch.update({name: vmem(dims, kind) for name in group.split()})
    for count, group in (
        (4, "load_sem sq_send sq_recv core_send core_recv db_send db_recv in_send in_recv in_local block_sem"),
        (messages, "x_send x_recv far_send far_recv relay_send relay_recv"), (6, "row_send row_recv total_sem"),
        (2, "y_send y_recv"), (8, "out_send out_recv out_local"), (1, "g_local o_local d_local c_local flag_local pair_send pair_recv intake_sem"),
        (planes, "g_right g_left g_sem o_right o_left o_sem d_send d_recv c_send c_recv flag_send flag_recv gain_send gain_recv"),
        (planes * chunks, "sum_right sum_left got_left got_right"), (SLOTS, "grad_sem"),
    ):
        scratch.update({name: pltpu.SemaphoreType.DMA((count,)) for name in group.split()})
    scratch["go_sem"] = pltpu.SemaphoreType.REGULAR((2,))
    results = pl.pallas_call(
        functools.partial(main_kernel, (*args, *outs, *scratch)),
        out_shape=tuple(outs.values()),
        in_specs=[places.get(name, ANY) for name in args],
        out_specs=tuple(places.get(name, ANY) for name in outs),
        scratch_shapes=list(scratch.values()),
        compiler_params=pltpu.CompilerParams(collective_id=1, has_side_effects=True, vmem_limit_bytes=VMEM_LIMIT),
        name="main",
    )(*args.values())
    return dict(zip(outs, results))


def local(inputs, cotangent, width_index, qkv_weight, out_weight, attn_gain, ffn_gain, up_weight, down_weight):
    found = run_main(width_index, inputs, cotangent, attn_gain, ffn_gain, qkv_weight, out_weight, up_weight, down_weight)
    gains = found["gain_grads"]
    size = gains.shape[1] // (2 * lax.axis_size("dp"))
    own = (lax.axis_index("dp") * 2 + lax.axis_index("mp")) * size
    gain_grads = lax.dynamic_slice_in_dim(gains[:2], own, size, axis=1)
    return (
        found["layer_out"][None],
        found["input_grad"][None],
        found["qkv_grad"],
        found["out_grad"],
        gain_grads[0],
        gain_grads[1],
        found["up_grad"],
        found["down_grad"],
    )


def solution(mesh):
    in_specs = (
        P("dp", "mp", None),
        P("dp", "mp", None),
        P("dp"),
        P(None, "section", "mp"),
        P("section", "mp"),
        P("section"),
        P("section"),
        P("section", "mp"),
        P("section", "mp"),
    )
    out_specs = (
        P("section", "dp", "mp", None),
        P("section", "dp", "mp", None),
        P(None, ("section", "dp"), "mp"),
        P(("section", "dp"), "mp"),
        P(("section", "dp", "mp")),
        P(("section", "dp", "mp")),
        P(("section", "dp"), "mp"),
        P(("section", "dp"), "mp"),
    )
    return jax.shard_map(local, mesh=mesh, in_specs=in_specs, out_specs=out_specs, check_vma=False)
```

time: 426 us -> 392 us (0.920)
  the two profiles are of different devices: /device:TPU:22 before, /device:TPU:15 now
where the time goes in v1:
time: 392 us; the launch traced here: 385 us
  Pallas kernels  374 us (95%)
  local copies, waits for them, and re-layouts  10.6 us (3%)
    pallas_call x1, Pallas kernels, run_main(): pl.pallas_call(functools.partial(main_kernel, (*args, *outs, *scratch)),...  374 us
    unnamed x14, local copies, waits for them, and re-layouts  9.18 us

profile of v1, /device:TPU:15, one launch (start us, length us, event | category | flops | bytes accessed | tf_op | source)
XLA Modules:
  0.0 385.1 jit_solution(8698854864178075076)
XLA Ops:
  0.6 373.7 %main.1 = (bf16[2,128,1536]{2,1,0:T(8,128)(2,1)}, bf16[2,128,1536]{2,1,0:T(8,128)(2,1)}, f32[3,192,768]{2,1,0:T(8,128)}, f32[192,768]{1,0:T(8,128)}, f32[192,307...) custom-call(s32[2]{0:T(128)} %refs_0_.1, ...), custom_call_target="tpu_custom_call" | custom-call | tf_op jit(solution)/shard_map/main/pallas_call | solution.py:1130
  374.3 0.0 copy-start.2
  374.3 0.9 slice.9
  375.2 0.1 constant_dynamic-slice_fusion
  375.2 0.5 slice_bitcast_fusion
  375.8 0.0 copy-start.3
  375.8 2.1 copy.25
  377.9 0.0 copy-start.1
  377.9 2.2 copy.26
  380.1 0.0 copy-done.2
  380.1 1.2 copy.27
  381.3 0.0 copy-done.3
  381.3 0.0 copy-start
  381.3 0.8 copy.28
  382.1 0.0 copy-done.1
  382.1 1.4 copy.29
  383.6 0.0 copy-done
  383.6 1.4 copy.30
Async XLA Ops:
  374.3 5.8 %copy-start.2 = (f32[3,192,768]{2,1,0:T(8,128)S(1)}, f32[3,192,768]{2,1,0:T(8,128)}, u32[]{:S(2)}) copy-start(f32[3,192,768]{2,1,0:T(8,128)} %get-tuple-element.34) | copy-start | bytes 5308420
  375.8 5.6 %copy-start.3 = (f32[192,768]{1,0:T(8,128)S(1)}, f32[192,768]{1,0:T(8,128)}, u32[]{:S(2)}) copy-start(f32[192,768]{1,0:T(8,128)} %get-tuple-element.35) | copy-start | bytes 1769476
  377.9 4.2 %copy-start.1 = (f32[192,3072]{1,0:T(8,128)S(1)}, f32[192,3072]{1,0:T(8,128)}, u32[]{:S(2)}) copy-start(f32[192,3072]{1,0:T(8,128)} %get-tuple-element.38) | copy-start | bytes 7077892
  381.3 2.2 copy-start

commit v2 on v1

--- a/solution.py
+++ b/solution.py
@@ -15,12 +15,13 @@
 GELU_A = 0.044715
 MESH = pl.DeviceIdType.MESH
 SLOTS = 10
-LAG = 5
-GRADS_TURN = 10
+AHEAD = 3
+SHARED = 6
 DIRECT_ROWS = 144
+URGENT_ROWS = 192
 F32 = jnp.float32
 BF16 = jnp.bfloat16
-VMEM_LIMIT = 62 * 2**20
+VMEM_LIMIT = 63 * 2**20
 
 
 def mm(a, b):
@@ -116,24 +117,34 @@
 
 
 class PairLink:
-    def __init__(self, place, relay, sems, targets):
+    def __init__(self, place, relay, sems, targets, urgent):
         self.place, self.relay, self.targets = place, relay, targets
         self.send, self.recv, self.far_send, self.far_recv, self.relay_send, self.relay_recv = sems
-        rows = DIRECT_ROWS + relay.shape[1]
-        self.direct = slice(0, DIRECT_ROWS)
-        self.detour = slice(DIRECT_ROWS, rows)
+        self.rows = DIRECT_ROWS + relay.shape[1]
+        self.urgent = urgent
         self.sources = {}
 
+    def direct(self, index):
+        return slice(0, URGENT_ROWS if index in self.urgent else DIRECT_ROWS)
+
+    def detour(self, index):
+        return slice(URGENT_ROWS if index in self.urgent else DIRECT_ROWS, self.rows)
+
+    def held(self, index):
+        rows = self.detour(index)
+        return self.relay.at[index, 0:rows.stop - rows.start]
+
     def near(self, index):
-        src, dst = self.sources[index](self.direct), self.targets(index, self.place.half, self.direct)
+        rows = self.direct(index)
+        src, dst = self.sources[index](rows), self.targets(index, self.place.half, rows)
         return remote(src, dst, self.send.at[index], self.recv.at[index], self.place.pair)
 
     def far(self, index):
-        src = self.sources[index](self.detour)
-        return remote(src, self.relay.at[index], self.far_send.at[index], self.relay_recv.at[index], self.place.across)
+        src = self.sources[index](self.detour(index))
+        return remote(src, self.held(index), self.far_send.at[index], self.relay_recv.at[index], self.place.across)
 
     def whole(self, index):
-        rows, src = slice(0, self.detour.stop), self.sources[index]
+        rows, src = slice(0, self.rows), self.sources[index]
         dst = self.targets(index, self.place.half, rows)
         return remote(src(rows), dst, self.send.at[index], self.recv.at[index], self.place.pair)
 
@@ -155,12 +166,12 @@
 
     def wait(self, index):
         other = 1 - self.place.half
-        for rows, sem in ((self.direct, self.recv), (self.detour, self.far_recv)):
+        for rows, sem in ((self.direct(index), self.recv), (self.detour(index), self.far_recv)):
             dst = self.targets(index, other, rows)
             remote(dst, dst, self.send.at[index], sem.at[index], self.place.pair).wait_recv()
 
     def wait_whole(self, index):
-        dst = self.targets(index, 1 - self.place.half, slice(0, self.detour.stop))
+        dst = self.targets(index, 1 - self.place.half, slice(0, self.rows))
         remote(dst, dst, self.send.at[index], self.recv.at[index], self.place.pair).wait_recv()
 
     def finish(self, indices):
@@ -172,16 +183,19 @@
         for index in indices:
             self.whole(index).wait_send()
 
+    def passed(self, index):
+        dst = self.targets(index, self.place.half, self.detour(index))
+        return remote(self.held(index), dst, self.relay_send.at[index], self.far_recv.at[index], self.place.corner)
+
     def forward(self, indices):
-        copies = []
         for index in indices:
-            held = self.relay.at[index]
+            held = self.held(index)
             remote(held, held, self.relay_send.at[index], self.relay_recv.at[index], self.place.across).wait_recv()
-            copy = remote(held, self.targets(index, self.place.half, self.detour), self.relay_send.at[index], self.far_recv.at[index], self.place.corner)
-            copy.start()
-            copies.append(copy)
-        for copy in copies:
-            copy.wait_send()
+            self.passed(index).start()
+
+    def finish_forward(self, indices):
+        for index in indices:
+            self.passed(index).wait_send()
 
 
 def spread(value, width):
@@ -261,11 +275,11 @@
 
 
 class Gather:
-    def __init__(self, place, mine, every, sems, first, last):
+    def __init__(self, place, mine, every, sems):
         self.me, self.count = lax.axis_index("dp"), lax.axis_size("dp")
         self.place, self.mine, self.every = place, mine, every
         self.right, self.left, self.recv, self.local = sems
-        self.first, self.last = first, min(last, self.count - 1)
+        self.last = self.count - 1
 
     def send(self, block, way, number):
         section, dp, mp = self.place.at
@@ -293,7 +307,7 @@
         for way, block, active in self.moves(number):
             @pl.when(active)
             def _(way=way, block=block):
-                if number > self.first:
+                if number > 1:
                     self.arrive(block)
                 self.send(block, way, number).start()
 
@@ -301,8 +315,8 @@
         for more in range(number, self.last + 1):
             self.step(more)
 
-    def finish(self):
-        for number in range(self.first, self.last + 1):
+    def settle(self, first, last):
+        for number in range(first, min(last, self.last) + 1):
             left, right = self.me - number, self.me + number
             done = number == self.last
 
@@ -314,33 +328,42 @@
             def _(block=right):
                 self.arrive(block)
 
+    def settle_all(self):
+        self.own().wait()
+        self.settle(1, self.last)
+
+    def finish(self):
+        for number in range(1, self.last + 1):
             for way, block, active in self.moves(number):
                 @pl.when(active)
                 def _(way=way, block=block):
                     self.send(block, way, number).wait_send()
-        if self.first == 1:
-            self.own().wait()
 
 
 class Scatter:
-    def __init__(self, place, piece, landing, sends, arrivals, slots, intake, in_sem, chunks):
-        self.place, self.piece, self.landing, self.sends, self.arrivals = place, piece, landing, sends, arrivals
+    def __init__(self, place, piece, which, total, landing, sends, arrivals, slots, places, intake, in_sem, chunks):
+        self.places = places
+        self.place, self.piece, self.which, self.total = place, piece, which, total
+        self.landing, self.sends, self.arrivals = landing, sends, arrivals
         self.slots, self.intake, self.in_sem, self.chunks = slots, intake, in_sem, chunks
         self.me, self.count = lax.axis_index("dp"), lax.axis_size("dp")
 
-    def send(self, way, target, chunk, src):
+    def send(self, way, target, number, src):
         section, dp, mp = self.place.at
-        at = target * self.chunks + chunk
-        return remote(src, self.landing[way].at[target, chunk], self.sends[way].at[at], self.arrivals[way].at[at], (section, dp + way, mp))
-
-    def fetch(self, way, target, chunk):
-        at = target * self.chunks + chunk
-        held = self.landing[way].at[target, chunk]
-        remote(held, held, self.sends[way].at[at], self.arrivals[way].at[at], self.place.pair).wait_recv()
-        copy = pltpu.make_async_copy(held, self.intake[way], self.in_sem.at[0])
-        copy.start()
-        copy.wait()
-        return self.intake[way][...].astype(F32)
+        dst = self.landing[way].at[target, number]
+        send_sem = self.sends[way].at[target * 4 + lax.rem(number, 4)]
+        return remote(src, dst, send_sem, self.arrivals[way].at[target * self.chunks + number], (section, dp + way, mp))
+
+    def own(self, number, target):
+        return self.piece(self.which(number), target)
+
+    def arrived(self, way, target, number):
+        held = self.landing[way].at[target, number]
+        got = self.arrivals[way].at[target * self.chunks + number]
+        remote(held, held, self.sends[way].at[0], got, self.place.pair).wait_recv()
+
+    def taken(self, way, target, number, buffer):
+        return pltpu.make_async_copy(self.landing[way].at[target, number], self.intake(buffer), self.in_sem.at[buffer])
 
     def each(self, way, body):
         def step_body(step, carry):
@@ -348,69 +371,109 @@
             return carry
         lax.fori_loop(0, self.count - 1, step_body, 0)
 
-    def from_edge(self, way, chunk):
-        @pl.when(self.me == (0 if way > 0 else self.count - 1))
-        def _():
-            self.each(way, lambda step, target: self.send(way, target, chunk, self.piece(chunk, target)).start())
-
-    def edges(self, chunk):
-        self.from_edge(1, chunk)
-        self.from_edge(-1, chunk)
+    def at_edge(self, way):
+        return self.me == (0 if way > 0 else self.count - 1)
+
+    def edges(self, number):
+        for way in (1, -1):
+            @pl.when(self.at_edge(way) & (number < self.total))
+            def _(way=way):
+                self.each(way, lambda step, target: self.send(way, target, number, self.own(number, target)).start())
 
     def between(self, way, target):
         if way > 0:
             return (self.me > 0) & (self.me < target)
         return (self.me < self.count - 1) & (self.me > target)
 
+    def staging(self, way):
+        live = jnp.maximum(self.count - 1 - self.me if way > 0 else self.me, 1)
+        return jnp.minimum(lax.div(self.places, live), 4), live
+
     def turns(self):
         return range(self.chunks + max(self.count - 3, 0))
 
-    def middle(self, turn):
+    def turn(self, turn):
+        if turn + AHEAD < self.chunks:
+            for way in (1, -1):
+                @pl.when(self.at_edge(way) & (turn + AHEAD < self.total))
+                def _(way=way):
+                    self.each(way, lambda step, target: self.send(way, target, turn, self.own(turn, target)).wait_send())
+            self.edges(turn + AHEAD)
         if self.count < 3 or turn not in self.turns():
             return
-        def pass_on(way, step, target):
+
+        ways = ((1, 0, lambda step: self.count - 1 - step), (-1, 1, lambda step: step))
+
+        def number_of(way, target):
             depth = self.me if way > 0 else self.count - 1 - self.me
-            chunk = turn + 1 - depth
-
-            @pl.when(self.between(way, target) & (chunk >= 0) & (chunk < self.chunks))
-            def _():
-                slot = self.slots(way, lax.rem(chunk, 2) * (self.count - 1) + step)
-                total = self.fetch(way, target, chunk) + self.piece(chunk, target)[...].astype(F32)
-
-                @pl.when(chunk >= 2)
-                def _():
-                    self.send(way, target, chunk - 2, slot).wait_send()
-
-                slot[...] = total.astype(BF16)
-                self.send(way, target, chunk, slot).start()
-
-        def both(step, carry):
-            pass_on(1, step, self.count - 1 - step)
-            pass_on(-1, step, step)
+            number = turn + 1 - depth
+            return number, self.between(way, target) & (number >= 0) & (number < self.total)
+
+        def take(step, carry):
+            for way, side, target_of in ways:
+                target = target_of(step)
+                number, active = number_of(way, target)
+
+                @pl.when(active)
+                def _(way=way, side=side, target=target, number=number):
+                    self.arrived(way, target, number)
+                    self.taken(way, target, number, 2 * step + side).start()
             return carry
 
-        lax.fori_loop(0, self.count - 1, both, 0)
-
-    def last(self, chunk, total_ref):
-        total_ref[...] = self.piece(chunk, self.me)[...].astype(F32)
-        for way, there in ((1, self.me > 0), (-1, self.me < self.count - 1)):
+        def pass_on(step, carry):
+            for way, side, target_of in ways:
+                target = target_of(step)
+                number, active = number_of(way, target)
+
+                @pl.when(active)
+                def _(way=way, side=side, target=target, number=number):
+                    depth, live = self.staging(way)
+                    slot = self.slots(way, lax.rem(number, depth) * live + step)
+                    buffer = 2 * step + side
+                    self.taken(way, target, number, buffer).wait()
+                    total = self.intake(buffer)[...].astype(F32) + self.own(number, target)[...].astype(F32)
+
+                    @pl.when(number >= depth)
+                    def _():
+                        self.send(way, target, number - depth, slot).wait_send()
+
+                    slot[...] = total.astype(BF16)
+                    self.send(way, target, number, slot).start()
+            return carry
+
+        lax.fori_loop(0, self.count - 1, take, 0)
+        lax.fori_loop(0, self.count - 1, pass_on, 0)
+
+    def last(self, number, total_ref):
+        ways = ((1, 0, self.me > 0), (-1, 1, self.me < self.count - 1))
+        for way, side, there in ways:
             @pl.when(there)
-            def _(way=way):
-                total_ref[...] = total_ref[...] + self.fetch(way, self.me, chunk)
+            def _(way=way, side=side):
+                self.arrived(way, self.me, number)
+                self.taken(way, self.me, number, side).start()
+        total_ref[...] = self.own(number, self.me)[...].astype(F32)
+        for way, side, there in ways:
+            @pl.when(there)
+            def _(way=way, side=side):
+                self.taken(way, self.me, number, side).wait()
+                total_ref[...] = total_ref[...] + self.intake(side)[...].astype(F32)
 
     def finish(self):
         for way in (1, -1):
-            edge = self.me == (0 if way > 0 else self.count - 1)
-
-            def sent(chunk, step, target, way=way, edge=edge):
-                active = (edge | self.between(way, target)) if chunk >= self.chunks - 2 else edge
-
-                @pl.when(active)
-                def _():
-                    self.send(way, target, chunk, self.piece(chunk, target)).wait_send()
-
-            for chunk in range(self.chunks):
-                self.each(way, functools.partial(sent, chunk))
+            depth, _ = self.staging(way)
+            for back in range(1, 5):
+                number = self.total - back
+
+                def sent(step, target, way=way, back=back, number=number, depth=depth):
+                    active = self.between(way, target) & (back <= depth)
+                    if back <= AHEAD:
+                        active = active | self.at_edge(way)
+
+                    @pl.when(active)
+                    def _():
+                        self.send(way, target, number, self.own(number, target)).wait_send()
+
+                self.each(way, sent)
 
 
 def main_kernel(names, *refs):
@@ -468,7 +531,7 @@
         n = index - first_dqkv
         return r.dqkv.at[n // 3, n % 3, rows, span]
 
-    link = PairLink(place, r.relay, (r.x_send, r.x_recv, r.far_send, r.far_recv, r.relay_send, r.relay_recv), targets)
+    link = PairLink(place, r.relay, (r.x_send, r.x_recv, r.far_send, r.far_recv, r.relay_send, r.relay_recv), targets, (6, 7, first_do, first_do + 1))
     forward_order = tuple(range(first_dg))
     ffn_order = tuple(range(first_dg, first_do))
     do_order = tuple(range(first_do, first_dqkv))
@@ -480,10 +543,18 @@
     def share_rows(n):
         return pl.ds(pl.multiple_of(n * share, share), share)
 
-    gather = Gather(place, r.g.at[0:SLOTS - 1], r.every_g, (r.g_right, r.g_left, r.g_sem, r.g_local), 1, length)
-    gather_o = Gather(place, r.o, r.every_o, (r.o_right, r.o_left, r.o_sem, r.o_local), 1, length)
+    gathers = [
+        Gather(
+            place, r.g.at[3 * n:3 * n + 3], r.every_g.at[n],
+            (r.g_right.at[n], r.g_left.at[n], r.g_sem.at[n], r.g_local.at[n:n + 1]),
+        )
+        for n in range(3)
+    ]
+    gather_o = Gather(place, r.o, r.every_o, (r.o_right, r.o_left, r.o_sem, r.o_local))
     exchange_d = Exchange(place, lambda n: r.dt.at[share_rows(n), :], r.every_d, (r.d_send, r.d_recv, r.d_local))
     exchange_c = Exchange(place, lambda n: r.dt.at[share_rows(n), :], r.every_c, (r.c_send, r.c_recv, r.c_local))
+    gather_u = Gather(place, r.du.at[SLOTS - SHARED:SLOTS], r.every_u, (r.u_right, r.u_left, r.u_sem, r.u_local))
+    exchange_b = Exchange(place, lambda n: r.dt.at[share_rows(n), 0:length], r.every_b, (r.b_send, r.b_recv, r.b_local))
     exchange_flag = Exchange(place, lambda n: r.wide, r.every_flag, (r.flag_send, r.flag_recv, r.flag_local))
     exchange_flag.start()
 
@@ -497,7 +568,7 @@
         return remote(r.x2.at[i], r.xa.at[i, my_rows, :], r.y_send.at[i], r.y_recv.at[i], place.across)
 
     def e_copy(i):
-        return remote(r.e_out.at[i], r.e_in.at[i, my_rows, :], r.y_send.at[i], r.y_recv.at[i], place.across)
+        return remote(r.x2.at[i], r.e_in.at[i, my_rows, :], r.y_send.at[i], r.y_recv.at[i], place.across)
 
     def start_half(src_ref, dst_ref, first):
         for i in range(seqs):
@@ -532,7 +603,7 @@
         return remote(r.snd_db.at[n], r.rcv_db.at[n], r.db_send.at[n], r.db_recv.at[n], place.core_peer)
 
     def da_rows(i):
-        return remote(r.snd_db.at[2 + i, their_rows, :], r.rcv_da.at[i], r.db_send.at[2 + i], r.db_recv.at[2 + i], place.core_peer)
+        return remote(r.snd_db.at[2 + i, their_rows, :], r.rcv_half.at[i], r.db_send.at[2 + i], r.db_recv.at[2 + i], place.core_peer)
 
     def ready(n):
         pl.semaphore_signal(r.go_sem.at[n], inc=1, device_id=place.pair, device_id_type=MESH)
@@ -734,34 +805,54 @@
     r.g[1] = r.g[1] + r.g[SLOTS - 1]
     finish_rows(1)
     emit_x2.prepare([r.x2[i] for i in range(seqs)])
-    gather.step(1)
-    gather_o.rest(3)
+    for part in gathers:
+        part.step(1)
+
+    def normed_again():
+        for i in range(seqs):
+            r.xg[i] = (r.xf[i].astype(F32) * r.rf[i][:, :1] * gain_f).astype(BF16)
+
+    @pl.when(place.block == 0)
+    def _():
+        normed_again()
+        r.dt[:, :length] = jnp.transpose(r.xg[1].astype(F32)).astype(BF16)
+        exchange_b.start()
 
     def piece(chunk, target):
         column = pl.multiple_of(lax.rem(chunk, 8) * unit, unit)
         return r.wud.at[lax.div(chunk, 8), share_rows(target), pl.ds(column, unit)]
 
+    per = max(length // share, 1)
+
     def slots(way, n):
-        per = max(length // share, 1)
         ref = r.snd_qkv if way > 0 else r.rcv_qkv
         at = lax.div(n, per)
         return ref.at[lax.div(at, 3), lax.rem(at, 3), share_rows(lax.rem(n, per)), :]
 
-    intake = {1: r.snd_u.at[0, 0:share, :], -1: r.snd_u.at[1, 0:share, :]}
+    def intake(n):
+        return r.snd_u.at[lax.div(n, per), share_rows(lax.rem(n, per)), :]
+
+    def which(number):
+        after = min(number // 2, 1) if isinstance(number, int) else jnp.minimum(lax.div(number, 2), 1)
+        return number + SHARED * after * (1 - place.block)
+
     scatter = Scatter(
-        place, piece, {1: r.from_left, -1: r.from_right}, {1: r.sum_right, -1: r.sum_left}, {1: r.got_left, -1: r.got_right},
-        slots, intake, r.intake_sem, 14,
+        place, piece, which, 14 - SHARED * (1 - place.block), {1: r.from_left, -1: r.from_right}, {1: r.sum_right, -1: r.sum_left}, {1: r.got_left, -1: r.got_right},
+        slots, 6 * per, intake, r.intake_sem, 14,
     )
 
     @pl.when(place.block == 0)
     def _():
+        gather_o.rest(3)
         link.forward(forward_order[3:first_u])
         link.forward(tuple(first_dg + slot for slot in DG_MIDDLE))
         link.forward(forward_order[first_u:])
-        gather.step(2)
+        for part in gathers:
+            part.step(2)
         link.forward(tuple(first_dg + slot for slot in DG_LATE))
         link.forward(do_order + dqkv_order)
-        gather.rest(3)
+        for part in gathers:
+            part.rest(3)
         for i, slot_list in enumerate((NARROW, WIDE)):
             e_copy(i).wait_recv()
             if i == 1:
@@ -779,6 +870,7 @@
                         link.start_far(first_dg + sent)
                 if i == 1 and slot > WIDE[1]:
                     link.start_far(first_dg + slot)
+        exchange_b.finish()
         transposed(r.e_in)
         exchange_d.start()
         link.finish(forward_order[:3])
@@ -788,8 +880,6 @@
         link.finish_whole(forward_order[:3])
 
     link.finish(forward_order[3:])
-    for i in range(seqs):
-        r.xg[i] = (r.xf[i].astype(F32) * r.rf[i][:, :1] * gain_f).astype(BF16)
 
     def hidden_back(slot):
         @pl.when(place.block == 0)
@@ -805,12 +895,18 @@
         r.du[slot] = du_k
         return mm_nt(du_k, slot_weight(slot, r.wu)), jnp.sum(du_k.astype(F32) * r.u[slot], axis=-1, keepdims=True)
 
-    def up_grad(block):
-        part = mm_tn(r.xg[1], r.du[2 + block])
-        if block < 2:
-            part = part + mm_tn(r.xg[0], r.du[block])
-        r.wu[:, block * unit:(block + 1) * unit] = part.astype(BF16)
-        scatter.edges(block)
+    def flipped(value):
+        return jnp.transpose(value.astype(F32)).astype(BF16)
+
+    def up_grads(blocks):
+        wide = flipped(r.xg[1])
+        for block in blocks:
+            part = mm(wide, r.du[2 + block])
+            if block < 2:
+                part = part + mm_tn(r.xg[0], r.du[block])
+            r.wu[:, block * unit:(block + 1) * unit] = part.astype(BF16)
+            if block < AHEAD:
+                scatter.edges(block)
 
     def core_sum_start(i, slot_list):
         total = row = None
@@ -818,10 +914,15 @@
             more, more_row = hidden_back(slot)
             total, row = (more, more_row) if total is None else (total + more, row + more_row)
 
-            if i == 1:
+            if i == 1 and slot - 2 < 8 - SHARED:
                 @pl.when(place.block == 0)
                 def _(slot=slot):
-                    up_grad(slot - 2)
+                    up_grads((slot - 2,))
+
+        if i == 1:
+            @pl.when(place.block == 0)
+            def _():
+                gather_u.step(1)
 
         r.snd_db[i] = total.astype(BF16)
         db_copy(i).start()
@@ -838,9 +939,10 @@
         new = r.e_in[i].astype(F32) + factor * (grad * gain_f - scaled * mean)
         r.e[i] = new
         r.dc[i] = new.astype(BF16)
-        r.snd_do[i] = mm(r.dc[i], r.wo[:, pl.ds(theirs, mine)]).astype(BF16)
-        link.start(first_do + i, lambda rows: r.snd_do.at[i, rows, :])
-        r.own_do[i] = mm(r.dc[i], r.wo[:, pl.ds(ours, mine)])
+        core_copy(i).wait_send()
+        r.snd_br[i, :, :mine] = mm(r.dc[i], r.wo[:, pl.ds(theirs, mine)]).astype(BF16)
+        link.start(first_do + i, lambda rows: r.snd_br.at[i, rows, 0:mine])
+        r.own_qkv[i, 0] = mm(r.dc[i], r.wo[:, pl.ds(ours, mine)])
         return jnp.sum(grad * scaled, axis=0, keepdims=True)
 
     core_sum_start(0, NARROW)
@@ -850,16 +952,74 @@
     r.gains[...] = jnp.zeros_like(r.gains)
     r.gains[1:2, :] = 0.5 * gain_f_sum
     emit_e1.prepare([r.dc[i, my_rows, :] for i in range(seqs)])
-    exchange_d.finish()
-    transposed(r.dc)
-    exchange_c.start()
+
+    @pl.when(place.block == 1)
+    def _():
+        exchange_d.finish()
+        transposed(r.dc)
+        exchange_c.start()
+
+    rows = slice(0, share)
+    inner = (me > 0) & (me < planes - 1)
+
+    def grads_ready():
+        exchange_flag.finish()
+        for n in range(SLOTS):
+            r.u[n, rows, :] = jnp.zeros_like(r.u[n, rows, :])
+        flags_copy = pltpu.make_async_copy(r.every_flag, r.flags, r.block_sem.at[0])
+        flags_copy.start()
+        flags_copy.wait()
+
+    def planes_of(part, first, last):
+        def body(k, carry):
+            part(jnp.where(me < planes // 2, lax.rem(me + k, planes), lax.rem(me + planes - k, planes)))
+            return carry
+        lax.fori_loop(lax.div(first * planes, 4), lax.div(last * planes, 4), body, 0)
+
+    def fetched(*pairs):
+        copies = [pltpu.make_async_copy(src, dst, r.block_sem.at[at]) for at, (src, dst) in enumerate(pairs)]
+        for copy in copies:
+            copy.start()
+        for copy in copies:
+            copy.wait()
+
+    def down_part(n):
+        block_g = r.snd_dg.at[0:SLOTS - 1]
+        fetched(*((r.every_g.at[k, n], r.snd_dg.at[3 * k:3 * k + 3]) for k in range(3)), (r.every_d.at[n], r.block_d))
+        on = r.flags[n][:1, :1]
+        shared = block_g[1].astype(F32)
+        upper, lower = (shared * on).astype(BF16), (shared * (1.0 - on)).astype(BF16)
+        narrow, wide = r.block_d[:, :length], r.block_d[:, length:]
+        for block in range(8):
+            right = upper if block == 4 else block_g[2 + block if block < 4 else 1 + block]
+            part = mm(wide, right)
+            if block < 2:
+                part = part + mm(narrow, block_g[0] if block == 0 else lower)
+            r.u[block, rows, :] = r.u[block, rows, :] + part
+
+    def out_part(n):
+        fetched((r.every_o.at[n], r.xf), (r.every_c.at[n], r.block_c))
+        for side in range(2):
+            span = slice(side * unit, (side + 1) * unit)
+            part = mm(r.block_c[:, :length], r.xf[0, :, span]) + mm(r.block_c[:, length:], r.xf[1, :, span])
+            r.u[8 + side, rows, :] = r.u[8 + side, rows, :] + part
+
+    def gather_done():
+        for part in gathers:
+            part.settle_all()
+
+    def up_part(n):
+        block_u, block_b = r.rcv_dg.at[0:SHARED], r.rcv_dg.at[SHARED, rows, 0:length]
+        fetched((r.every_u.at[n], block_u), (r.every_b.at[n], block_b))
+        for k in range(SHARED):
+            r.own_qkv[k // 3, k % 3, rows, :] = r.own_qkv[k // 3, k % 3, rows, :] + mm(block_b[...], block_u[k])
 
     for i in range(seqs):
         link.wait(first_do + i)
         row = jnp.zeros((length, 1), F32)
         for j in range(z.heads):
             span = pl.ds(j * HEAD_DIM, HEAD_DIM)
-            do_j = (r.own_do[i, :, span] + r.rcv_do[i, :, span].astype(F32)).astype(BF16)
+            do_j = (r.own_qkv[i, 0, :, span] + r.rcv_do[i, :, span].astype(F32)).astype(BF16)
             q_j, k_j, v_j, probs = r.q[i, :, span], r.k[i, :, span], r.v[i, :, span], r.p[i, j]
             dp = mm_nt(do_j, v_j)
             dv = mm_tn(probs.astype(BF16), do_j)
@@ -875,17 +1035,27 @@
         row_copy(2 + i, place.pair).start()
         for t in range(3):
             link.start(first_dqkv + 3 * i + t, lambda rows, i=i, t=t: r.dqkv.at[i, t, rows, pl.ds(ours, mine)])
-        if i == 0:
+
+    def first_grads():
+        link.finish_whole(ffn_order[:len(NARROW)])
+        link.finish(ffn_order[len(NARROW):])
+        exchange_d.finish()
+        transposed(r.dc)
+        exchange_c.start()
+        grads_ready()
+        gather_done()
+
+    @pl.when((place.block == 0) & inner)
+    def _():
+        first_grads()
+        planes_of(down_part, 0, 1)
+
+    for i in range(seqs):
+        if i == 1:
             @pl.when(place.block == 0)
             def _():
-                scatter.middle(0)
-
-    @pl.when(place.block == 0)
-    def _():
-        for chunk in range(1, 4):
-            scatter.middle(chunk)
-
-    for i in range(seqs):
+                gather_u.step(2)
+
         part = jnp.zeros((length, feats), F32)
         for t in range(3):
             link.wait(first_dqkv + 3 * i + t)
@@ -896,16 +1066,21 @@
         r.snd_row[4 + i] = r.snd_row[2 + i] + r.rcv_row[2 + i]
         row_copy(4 + i, place.core_peer).start()
 
+    @pl.when(place.block == 0)
+    def _():
+        for i in range(seqs):
+            x_copy(i).wait_send()
+
     gain_a_sum = jnp.zeros((1, feats), F32)
     for i in range(seqs):
         da_rows(i).wait_recv()
         row_copy(4 + i, place.core_peer).wait_recv()
         r.snd_row[6 + i] = (r.snd_row[4 + i] + r.rcv_row[4 + i]) * (1.0 / z.width)
         mean = from_row(r.snd_row[6 + i, :, my_rows])
-        grad = r.snd_db[2 + i, my_rows, :].astype(F32) + r.rcv_da[i].astype(F32)
+        grad = r.snd_db[2 + i, my_rows, :].astype(F32) + r.rcv_half[i].astype(F32)
         factor = r.ra[i, my_rows, :][:, :1]
         scaled = r.xa[i, my_rows, :].astype(F32) * factor
-        r.e_out[i] = (r.e[i, my_rows, :] + factor * (grad * gain_a - scaled * mean)).astype(BF16)
+        r.x2[i] = (r.e[i, my_rows, :] + factor * (grad * gain_a - scaled * mean)).astype(BF16)
         gain_a_sum = gain_a_sum + jnp.sum(grad * scaled, axis=0, keepdims=True)
 
         @pl.when(place.block == 1)
@@ -913,33 +1088,64 @@
             e_copy(i).start()
 
     r.gains[0:1, :] = gain_a_sum
-    emit_e0.prepare([r.e_out[i] for i in range(seqs)])
+    emit_e0.prepare([r.x2[i] for i in range(seqs)])
 
     def qkv_grad():
         for i in range(seqs):
             r.xg[i] = (r.xa[i].astype(F32) * r.ra[i][:, :1] * gain_a).astype(BF16)
+        first, second = flipped(r.xg[0]), flipped(r.xg[1])
         for t in range(3):
-            r.wd[:, t * z.cols:(t + 1) * z.cols] = (mm_tn(r.xg[0], r.dqkv[0, t]) + mm_tn(r.xg[1], r.dqkv[1, t])).astype(BF16)
-            for chunk in range(8 + 2 * t, 10 + 2 * t):
-                scatter.edges(chunk)
+            r.wd[:, t * z.cols:(t + 1) * z.cols] = (mm(first, r.dqkv[0, t]) + mm(second, r.dqkv[1, t])).astype(BF16)
 
     @pl.when(place.block == 1)
     def _():
-        gather.step(2)
-        for block in range(8):
-            up_grad(block)
+        gather_o.rest(3)
+        for part in gathers:
+            part.step(2)
+        normed_again()
+        up_grads(range(8))
         qkv_grad()
         link.forward(ffn_order[len(NARROW):])
+        scatter.turn(0)
         link.forward(do_order)
-        gather.rest(3)
-        scatter.middle(0)
         link.forward(dqkv_order)
-        for chunk in range(1, 4):
-            scatter.middle(chunk)
+        scatter.turn(1)
+        gathers[0].rest(3)
+        scatter.turn(2)
+        scatter.turn(3)
+        gathers[1].rest(3)
 
     @pl.when(place.block == 0)
     def _():
         qkv_grad()
+        scatter.edges(2)
+
+        @pl.when(jnp.logical_not(inner))
+        def _():
+            first_grads()
+            planes_of(down_part, 0, 4)
+
+        @pl.when(inner)
+        def _():
+            planes_of(down_part, 1, 4)
+
+        gather_o.settle_all()
+        gather_u.own().wait()
+        gather_u.rest(3)
+        for k in range(SHARED):
+            r.own_qkv[k // 3, k % 3, rows, :] = jnp.zeros_like(r.own_qkv[k // 3, k % 3, rows, :])
+        for turn in range(4):
+            scatter.turn(turn)
+
+            @pl.when(inner)
+            def _(turn=turn):
+                planes_of(up_part, turn, turn + 1)
+
+    @pl.when(place.block == 1)
+    def _():
+        link.finish_whole(tuple(first_dg + slot for slot in DG_STRAIGHT))
+        link.finish(tuple(first_dg + slot for slot in DG_MIDDLE + DG_LATE))
+        grads_ready()
 
     emit_x1.start(0)
     emit_x2.start(1)
@@ -947,80 +1153,120 @@
     emit_e0.start(0)
     gains_copy = remote(r.gains, r.core_gains, r.pair_send.at[0], r.pair_recv.at[0], place.core_peer)
     gains_copy.start()
-    exchange_flag.finish()
-    scatter.middle(4)
+    scatter.turn(4)
     gains_copy.wait()
     r.every_gain[me] = r.gains[...] + r.core_gains[...]
     exchange_gain = Exchange(place, lambda n: r.every_gain.at[me], r.every_gain, (r.gain_send, r.gain_recv, None))
     for n in range(1, planes):
         exchange_gain.copy(n).start()
 
-    rows = slice(0, share)
-    for n in range(SLOTS):
-        r.u[n, rows, :] = jnp.zeros_like(r.u[n, rows, :])
-    flags_copy = pltpu.make_async_copy(r.every_flag, r.flags, r.block_sem.at[0])
-    flags_copy.start()
-    flags_copy.wait()
-
-    def plane_grads(n, carry):
-        block_g = r.du.at[0:SLOTS - 1]
-        sources = ((r.every_g, block_g), (r.every_o, r.xf), (r.every_d, r.block_d), (r.every_c, r.block_c))
-        copies = [pltpu.make_async_copy(src.at[n], dst, r.block_sem.at[at]) for at, (src, dst) in enumerate(sources)]
-        for copy in copies:
-            copy.start()
-        for copy in copies:
-            copy.wait()
-        on = r.flags[n][:1, :1]
-        shared = block_g[1].astype(F32)
-        upper, lower = (shared * on).astype(BF16), (shared * (1.0 - on)).astype(BF16)
-        narrow, wide = r.block_d[:, :length], r.block_d[:, length:]
-        for block in range(8):
-            right = upper if block == 4 else block_g[2 + block if block < 4 else 1 + block]
-            part = mm(wide, right)
-            if block < 2:
-                part = part + mm(narrow, block_g[0] if block == 0 else lower)
-            r.u[block, rows, :] = r.u[block, rows, :] + part
-        for side in range(2):
-            span = slice(side * unit, (side + 1) * unit)
-            part = mm(r.block_c[:, :length], r.xf[0, :, span]) + mm(r.block_c[:, length:], r.xf[1, :, span])
-            r.u[8 + side, rows, :] = r.u[8 + side, rows, :] + part
-        return carry
-
     def grad_copy(n):
         dst = r.down_grad.at[:, n * unit:(n + 1) * unit] if n < 8 else r.out_grad.at[:, (n - 8) * unit:(n - 7) * unit]
         return pltpu.make_async_copy(r.u.at[n, rows, :], dst, r.grad_sem.at[n])
 
-    def total_slot(chunk):
-        at = chunk % 6
-        return r.own_qkv.at[at // 3, at % 3, rows, :]
-
-    def total_copy(chunk):
-        if chunk < 8:
-            dst = r.up_grad.at[:, chunk * unit:(chunk + 1) * unit]
-        else:
-            t, side = (chunk - 8) // 2, (chunk - 8) % 2
-            dst = r.qkv_grad.at[t, :, side * unit:(side + 1) * unit]
-        return pltpu.make_async_copy(total_slot(chunk), dst, r.total_sem.at[chunk % 6])
-
-    def final(chunk):
-        if chunk >= 6:
-            total_copy(chunk - 6).wait()
-        scatter.last(chunk, total_slot(chunk))
-        total_copy(chunk).start()
-
-    for turn in range(5, 14 + LAG):
-        scatter.middle(turn)
-        if turn >= LAG:
-            final(turn - LAG)
-        if turn == GRADS_TURN:
-            gather.finish()
-            gather_o.finish()
-            exchange_c.finish()
-            lax.fori_loop(0, planes, plane_grads, 0)
-            for n in range(SLOTS):
-                grad_copy(n).start()
-    for turn in range(14 + LAG, len(scatter.turns())):
-        scatter.middle(turn)
+    def shared_copy(k):
+        dst = r.up_grad.at[:, (8 - SHARED + k) * unit:(9 - SHARED + k) * unit]
+        return pltpu.make_async_copy(r.own_qkv.at[k // 3, k % 3, rows, :], dst, r.shared_sem.at[k])
+
+    def total_slot(number):
+        at = lax.rem(number, 4)
+        column = pl.multiple_of(lax.rem(at, 2) * unit, unit)
+        return r.e.at[lax.div(at, 2), rows, pl.ds(column, unit)]
+
+    def total_copy(number, action):
+        chunk = which(number)
+        src, sem = total_slot(number), r.total_sem.at[lax.rem(number, 4)]
+
+        @pl.when(chunk < 8)
+        def _():
+            dst = r.up_grad.at[:, pl.ds(pl.multiple_of(chunk * unit, unit), unit)]
+            action(pltpu.make_async_copy(src, dst, sem))
+
+        @pl.when(chunk >= 8)
+        def _():
+            column = pl.multiple_of(lax.rem(chunk, 2) * unit, unit)
+            dst = r.qkv_grad.at[lax.div(chunk - 8, 2), :, pl.ds(column, unit)]
+            action(pltpu.make_async_copy(src, dst, sem))
+
+    def final(number, carry):
+        @pl.when(number >= 4)
+        def _():
+            total_copy(number - 4, lambda copy: copy.wait())
+
+        scatter.last(number, total_slot(number))
+        total_copy(number, lambda copy: copy.start())
+        return carry
+
+    finals = (
+        {5: 3, 6: 5, 7: 6, 8: 7, 9: 8},
+        {5: 1, 6: 2, 7: 3, 8: 4, 9: 5, 10: 6, 11: 7, 12: 9, 13: 11, 14: 13, 15: 14},
+        {11: 8, 12: 10, 13: 11, 14: 13, 15: 14},
+    )
+
+    def finals_by(turn):
+        first, inside, outside = (max([count for at, count in table.items() if at <= turn], default=0) for table in finals)
+        return jnp.where(place.block == 0, first, jnp.where(inner, inside, outside))
+
+    def once(block, where, body):
+        pl.when((place.block == block) & (inner if where else jnp.logical_not(inner)))(body)
+
+    def all_planes(*parts):
+        for part in parts:
+            planes_of(part, 0, 4)
+
+    def edge_parts():
+        gather_u.settle(1, gather_u.last - 1)
+        planes_of(up_part, 0, 3)
+        exchange_c.finish()
+        planes_of(out_part, 0, 4)
+        gather_u.settle(gather_u.last, gather_u.last)
+        planes_of(up_part, 3, 4)
+
+    def late_edge_parts():
+        gather_done()
+        gather_o.settle_all()
+        exchange_c.finish()
+        all_planes(down_part, out_part)
+
+    def inner_start():
+        gather_done()
+        gather_o.settle_all()
+        exchange_c.finish()
+
+    def out_start():
+        exchange_c.finish()
+        planes_of(out_part, 0, 2)
+
+    for turn in range(5, max(16, len(scatter.turns()))):
+        scatter.turn(turn)
+        if turn == 5:
+            once(0, False, edge_parts)
+        if turn == 12:
+            once(1, False, late_edge_parts)
+        lax.fori_loop(finals_by(turn - 1), finals_by(turn), final, 0)
+        if turn == 5:
+            pl.when(place.block == 1)(lambda: gathers[2].rest(3))
+            once(0, True, out_start)
+        if turn == 6:
+            once(0, True, lambda: planes_of(out_part, 2, 4))
+        if turn == 7:
+            once(1, True, inner_start)
+        if 7 <= turn < 11:
+            once(1, True, lambda turn=turn: planes_of(down_part, turn - 7, turn - 6))
+        if turn == 7:
+            @pl.when(place.block == 0)
+            def _():
+                for n in range(SLOTS):
+                    grad_copy(n).start()
+                for k in range(SHARED):
+                    shared_copy(k).start()
+        if turn == 11:
+            once(1, True, lambda: planes_of(out_part, 0, 4))
+        if turn == 12:
+            @pl.when(place.block == 1)
+            def _():
+                for n in range(SLOTS):
+                    grad_copy(n).start()
     for n in range(1, planes):
         source = lax.rem(me + planes - n, planes)
         slot = r.every_gain.at[source]
@@ -1032,14 +1278,19 @@
     r.gain_grads[...] = gain_total
 
     scatter.finish()
-    for chunk in range(8, 14):
-        total_copy(chunk).wait()
+    for back in range(1, 5):
+        total_copy(scatter.total - back, lambda copy: copy.wait())
+
+    @pl.when(place.block == 0)
+    def _():
+        for k in range(SHARED):
+            shared_copy(k).wait()
+
     for n in range(SLOTS):
         grad_copy(n).wait()
     for n in range(4):
         sq_copy(n).wait_send()
     for i in range(seqs):
-        core_copy(i).wait_send()
         core_rows(i).wait_send()
         row_copy(i, place.core_peer).wait_send()
         row_copy(2 + i, place.pair).wait_send()
@@ -1050,18 +1301,17 @@
 
     @pl.when(place.block == 0)
     def _():
-        link.finish_whole(ffn_order[:len(NARROW)])
-        link.finish(ffn_order[len(NARROW):])
-        for i in range(seqs):
-            x_copy(i).wait_send()
+        link.finish_forward(forward_order[3:] + tuple(first_dg + slot for slot in DG_MIDDLE + DG_LATE) + do_order + dqkv_order)
 
     @pl.when(place.block == 1)
     def _():
-        link.finish_whole(tuple(first_dg + slot for slot in DG_STRAIGHT))
-        link.finish(tuple(first_dg + slot for slot in DG_MIDDLE + DG_LATE))
+        link.finish_forward(forward_order + ffn_order[len(NARROW):] + do_order + dqkv_order)
         for i in range(seqs):
             e_copy(i).wait_send()
 
+    for part in (*gathers, gather_o):
+        part.finish()
+    pl.when(place.block == 0)(gather_u.finish)
     emit_x1.finish(0)
     emit_x2.finish(1)
     emit_e1.finish(1)
@@ -1097,8 +1347,9 @@
         "layer_out": shape((seqs, tokens, width), BF16), "input_grad": shape((seqs, tokens, width), BF16),
         "qkv_grad": shape((3, share, z.cols), F32), "out_grad": shape((share, z.cols), F32),
         "up_grad": shape((share, 8 * z.unit), F32), "down_grad": shape((share, 8 * z.unit), F32), "gain_grads": shape(row, F32),
-        "every_g": shape((planes, SLOTS - 1, z.length, z.unit), BF16), "every_o": shape((planes, seqs, z.length, z.cols), BF16),
+        "every_g": shape((3, planes, 3, z.length, z.unit), BF16), "every_o": shape((planes, seqs, z.length, z.cols), BF16),
         "every_d": shape((planes, share, seqs * z.length), BF16), "every_c": shape((planes, share, seqs * z.length), BF16),
+        "every_u": shape((planes, SHARED, z.length, z.unit), BF16), "every_b": shape((planes, share, z.length), BF16),
         "every_flag": shape((planes, 8, 128), F32),
         "from_left": shape((planes, chunks, share, z.unit), BF16), "from_right": shape((planes, chunks, share, z.unit), BF16),
     }
@@ -1107,8 +1358,8 @@
     small, factor, pair = (8, 8, z.length), (seqs, z.length, 128), (4, z.length, z.feats)
     scratch = {"wqkv": vmem(wqkv.shape, BF16), "wo": vmem(wo.shape, BF16), "wud": vmem((2, *wu.shape), BF16)}
     for dims, kind, group in (
-        (state, BF16, "xa xf xg e_in dc"), (state, F32, "e"), (half_state, BF16, "x2 e_out rcv_half rcv_da"),
-        (heads_state, BF16, "q k v snd_do rcv_do"), (heads_state, F32, "own_do"),
+        (state, BF16, "xa xf xg e_in dc"), (state, F32, "e"), (half_state, BF16, "x2 rcv_half"),
+        (heads_state, BF16, "q k v rcv_do"),
         ((seqs, z.heads, z.length, z.length), F32, "p"), ((seqs, z.length, z.cols), BF16, "o"), (factor, F32, "ra rf"),
         (slots, F32, "u"), (slots, BF16, "g snd_u rcv_u du snd_dg rcv_dg"), (qkv, F32, "own_qkv"), (qkv, BF16, "snd_qkv rcv_qkv"),
         ((4, 8, z.length), F32, "snd_sq rcv_sq"), (small, F32, "snd_row rcv_row"), (pair, BF16, "snd_br snd_db"),
@@ -1121,11 +1372,14 @@
     for count, group in (
         (4, "load_sem sq_send sq_recv core_send core_recv db_send db_recv in_send in_recv in_local block_sem"),
         (messages, "x_send x_recv far_send far_recv relay_send relay_recv"), (6, "row_send row_recv total_sem"),
-        (2, "y_send y_recv"), (8, "out_send out_recv out_local"), (1, "g_local o_local d_local c_local flag_local pair_send pair_recv intake_sem"),
-        (planes, "g_right g_left g_sem o_right o_left o_sem d_send d_recv c_send c_recv flag_send flag_recv gain_send gain_recv"),
-        (planes * chunks, "sum_right sum_left got_left got_right"), (SLOTS, "grad_sem"),
+        (2, "y_send y_recv"), (8, "out_send out_recv out_local"), (1, "o_local d_local c_local flag_local pair_send pair_recv"),
+        (planes, "o_right o_left o_sem d_send d_recv c_send c_recv flag_send flag_recv gain_send gain_recv"),
+        (2 * planes, "intake_sem"), (planes * chunks, "got_left got_right"), (4 * planes, "sum_right sum_left"), (SHARED, "shared_sem"),
+        (planes, "u_right u_left u_sem b_send b_recv"), (1, "u_local b_local"), (SLOTS, "grad_sem"),
     ):
         scratch.update({name: pltpu.SemaphoreType.DMA((count,)) for name in group.split()})
+    scratch["g_local"] = pltpu.SemaphoreType.DMA((3,))
+    scratch.update({name: pltpu.SemaphoreType.DMA((3, planes)) for name in ("g_right", "g_left", "g_sem")})
     scratch["go_sem"] = pltpu.SemaphoreType.REGULAR((2,))
     results = pl.pallas_call(
         functools.partial(main_kernel, (*args, *outs, *scratch)),

time: 392 us -> 362 us (0.923)
  the two profiles are of different devices: /device:TPU:15 before, /device:TPU:0 now
where the time goes in v2:
time: 362 us; the launch traced here: 356 us
  Pallas kernels  345 us (95%)
  local copies, waits for them, and re-layouts  10.6 us (3%)
    pallas_call x1, Pallas kernels, run_main(): pl.pallas_call(functools.partial(main_kernel, (*args, *outs, *scratch)),...  345 us
    unnamed x14, local copies, waits for them, and re-layouts  9.18 us

profile of v2, /device:TPU:0, one launch (start us, length us, event | category | flops | bytes accessed | tf_op | source)
XLA Modules:
  0.0 356.5 jit_solution(7056920832501220479)
XLA Ops:
  0.6 345.0 %main.1 = (bf16[2,128,1536]{2,1,0:T(8,128)(2,1)}, bf16[2,128,1536]{2,1,0:T(8,128)(2,1)}, f32[3,192,768]{2,1,0:T(8,128)}, f32[192,768]{1,0:T(8,128)}, f32[192,307...) custom-call(s32[2]{0:T(128)} %refs_0_.1, ...), custom_call_target="tpu_custom_call" | custom-call | tf_op jit(solution)/shard_map/main/pallas_call | solution.py:1384
  345.6 0.0 copy-start.2
  345.6 0.9 slice.9
  346.5 0.1 constant_dynamic-slice_fusion
  346.6 0.5 slice_bitcast_fusion
  347.1 0.0 copy-start.3
  347.1 2.1 copy.25
  349.2 0.0 copy-start.1
  349.2 2.2 copy.26
  351.4 0.0 copy-done.2
  351.4 1.2 copy.27
  352.6 0.0 copy-done.3
  352.6 0.0 copy-start
  352.6 0.8 copy.28
  353.5 0.0 copy-done.1
  353.5 1.4 copy.29
  354.9 0.0 copy-done
  354.9 1.4 copy.30
Async XLA Ops:
  345.6 5.8 %copy-start.2 = (f32[3,192,768]{2,1,0:T(8,128)S(1)}, f32[3,192,768]{2,1,0:T(8,128)}, u32[]{:S(2)}) copy-start(f32[3,192,768]{2,1,0:T(8,128)} %get-tuple-element.34) | copy-start | bytes 5308420
  347.1 5.6 %copy-start.3 = (f32[192,768]{1,0:T(8,128)S(1)}, f32[192,768]{1,0:T(8,128)}, u32[]{:S(2)}) copy-start(f32[192,768]{1,0:T(8,128)} %get-tuple-element.35) | copy-start | bytes 1769476
  349.2 4.2 %copy-start.1 = (f32[192,3072]{1,0:T(8,128)S(1)}, f32[192,3072]{1,0:T(8,128)}, u32[]{:S(2)}) copy-start(f32[192,3072]{1,0:T(8,128)} %get-tuple-element.38) | copy-start | bytes 7077892
  352.6 2.2 copy-start

commit v3 on v2

--- a/solution.py
+++ b/solution.py
@@ -16,7 +16,7 @@
 MESH = pl.DeviceIdType.MESH
 SLOTS = 10
 AHEAD = 3
-SHARED = 6
+SHARED = 3
 DIRECT_ROWS = 144
 URGENT_ROWS = 192
 F32 = jnp.float32
@@ -833,7 +833,8 @@
         return r.snd_u.at[lax.div(n, per), share_rows(lax.rem(n, per)), :]
 
     def which(number):
-        after = min(number // 2, 1) if isinstance(number, int) else jnp.minimum(lax.div(number, 2), 1)
+        first = 8 - SHARED
+        after = min(number // first, 1) if isinstance(number, int) else jnp.minimum(lax.div(number, first), 1)
         return number + SHARED * after * (1 - place.block)
 
     scatter = Scatter(
@@ -1118,7 +1119,8 @@
     @pl.when(place.block == 0)
     def _():
         qkv_grad()
-        scatter.edges(2)
+        for number in range(8 - SHARED, AHEAD):
+            scatter.edges(number)
 
         @pl.when(jnp.logical_not(inner))
         def _():
@@ -1198,7 +1200,7 @@
         return carry
 
     finals = (
-        {5: 3, 6: 5, 7: 6, 8: 7, 9: 8},
+        {5: 3, **{turn: turn - 1 for turn in range(6, 16 - SHARED)}},
         {5: 1, 6: 2, 7: 3, 8: 4, 9: 5, 10: 6, 11: 7, 12: 9, 13: 11, 14: 13, 15: 14},
         {11: 8, 12: 10, 13: 11, 14: 13, 15: 14},
     )
@@ -1275,7 +1277,8 @@
     gain_total = r.every_gain[0]
     for n in range(1, planes):
         gain_total = gain_total + r.every_gain[n]
-    r.gain_grads[...] = gain_total
+    own_first = (place.at[1] * 2 + core) * (feats // (2 * planes))
+    r.gain_grads[...] = pltpu.roll(gain_total, lax.rem(feats - own_first, feats), 1)
 
     scatter.finish()
     for back in range(1, 5):
@@ -1393,21 +1396,51 @@
     return dict(zip(outs, results))
 
 
+OUTPUTS = ("layer_out", "input_grad", "qkv_grad", "out_grad", "up_grad", "down_grad")
+PARTS = 2
+
+
+def deliver_kernel(*refs):
+    count = len(OUTPUTS)
+    gains, sources, (attn_out, ffn_out), targets = refs[0], refs[1:1 + count], refs[1 + count:3 + count], refs[3 + count:3 + 2 * count]
+    held, load_sem, save_sem = refs[3 + 2 * count:-2], refs[-2], refs[-1]
+    loads, saves = [], []
+    for n, (src, mid, dst) in enumerate(zip(sources, held, targets)):
+        rows = src.shape[-2] // PARTS
+        lead = (slice(None),) * (len(src.shape) - 2)
+        for part in range(PARTS):
+            at = (*lead, slice(part * rows, (part + 1) * rows))
+            loads.append(pltpu.make_async_copy(src.at[at], mid.at[at], load_sem.at[n * PARTS + part]))
+            saves.append(pltpu.make_async_copy(mid.at[at], dst.at[at], save_sem.at[n * PARTS + part]))
+    for copy in loads:
+        copy.start()
+    size = attn_out.shape[1]
+    attn_out[...] = gains[0:1, :size]
+    ffn_out[...] = gains[1:2, :size]
+    for load, copy in zip(loads, saves):
+        load.wait()
+        copy.start()
+    for copy in saves:
+        copy.wait()
+
+
 def local(inputs, cotangent, width_index, qkv_weight, out_weight, attn_gain, ffn_gain, up_weight, down_weight):
     found = run_main(width_index, inputs, cotangent, attn_gain, ffn_gain, qkv_weight, out_weight, up_weight, down_weight)
-    gains = found["gain_grads"]
-    size = gains.shape[1] // (2 * lax.axis_size("dp"))
-    own = (lax.axis_index("dp") * 2 + lax.axis_index("mp")) * size
-    gain_grads = lax.dynamic_slice_in_dim(gains[:2], own, size, axis=1)
+    sources = [found[name] for name in OUTPUTS]
+    size = attn_gain.shape[0] // (2 * lax.axis_size("dp"))
+    gain = jax.ShapeDtypeStruct((1, size), F32)
+    attn_grad, ffn_grad, *results = pl.pallas_call(
+        deliver_kernel,
+        out_shape=(gain, gain, *(jax.ShapeDtypeStruct(source.shape, source.dtype) for source in sources)),
+        in_specs=[IN_VMEM] + [ANY] * len(sources),
+        out_specs=(IN_VMEM, IN_VMEM, *[ANY] * len(sources)),
+        scratch_shapes=[vmem(source.shape, source.dtype) for source in sources] + [pltpu.SemaphoreType.DMA((len(sources) * PARTS,))] * 2,
+        compiler_params=pltpu.CompilerParams(vmem_limit_bytes=VMEM_LIMIT),
+        name="deliver",
+    )(found["gain_grads"], *sources)
+    layer_out, input_grad, qkv_grad, out_grad, up_grad, down_grad = results
     return (
-        found["layer_out"][None],
-        found["input_grad"][None],
-        found["qkv_grad"],
-        found["out_grad"],
-        gain_grads[0],
-        gain_grads[1],
-        found["up_grad"],
-        found["down_grad"],
+        layer_out[None], input_grad[None], qkv_grad, out_grad, attn_grad.reshape(size), ffn_grad.reshape(size), up_grad, down_grad,
     )
 
 

time: 362 us -> 353 us (0.975)
  local copies, waits for them, and re-layouts: 10.6 us -> 0 us
    unnamed x14 -> x0, local copies, waits for them, and re-layouts: 9.18 us -> none
    pallas_call x0 -> x1, Pallas kernels: none -> 7.84 us  [local(): pl.pallas_call(deliver_kernel, out_shape=(gain, gain, *(jax.ShapeDtypeStr...]
    pallas_call x1, Pallas kernels: 345 us -> 339 us  [run_main(): pl.pallas_call(functools.partial(main_kernel, (*args, *outs, *scratch)),...]
where the time goes in v3:
time: 353 us; the launch traced here: 347 us
  Pallas kernels  346 us (98%)
    pallas_call x1, Pallas kernels, run_main(): pl.pallas_call(functools.partial(main_kernel, (*args, *outs, *scratch)),...  339 us
    pallas_call x1, Pallas kernels, local(): pl.pallas_call(deliver_kernel, out_shape=(gain, gain, *(jax.ShapeDtypeStr...  7.84 us

profile of v3, /device:TPU:0, one launch (start us, length us, event | category | flops | bytes accessed | tf_op | source)
XLA Modules:
  0.0 347.3 jit_solution(12392076568379574896)
XLA Ops:
  0.6 338.6 %main.1 = (bf16[2,128,1536]{2,1,0:T(8,128)(2,1)}, bf16[2,128,1536]{2,1,0:T(8,128)(2,1)}, f32[3,192,768]{2,1,0:T(8,128)}, f32[192,768]{1,0:T(8,128)}, f32[192,307...) custom-call(s32[2]{0:T(128)} %refs_0_.1, ...), custom_call_target="tpu_custom_call" | custom-call | tf_op jit(solution)/shard_map/main/pallas_call | solution.py:1387
  339.2 7.8 %deliver.1 = (f32[1,96]{1,0:T(1,128)}, f32[1,96]{1,0:T(1,128)}, bf16[2,128,1536]{2,1,0:T(8,128)(2,1)}, bf16[2,128,1536]{2,1,0:T(8,128)(2,1)}, f32[3,192,768]{2,1...) custom-call(f32[8,768]{1,0:T(8,128)} %get-tuple-element.23.refs_0_, ...), custom_call_target="tpu_custom_call" | custom-call | tf_op jit(solution)/shard_map/deliver/pallas_call | solution.py:1432

commit v4 on v3

--- a/solution.py
+++ b/solution.py
@@ -1133,11 +1133,12 @@
 
         gather_o.settle_all()
         gather_u.own().wait()
-        gather_u.rest(3)
         for k in range(SHARED):
             r.own_qkv[k // 3, k % 3, rows, :] = jnp.zeros_like(r.own_qkv[k // 3, k % 3, rows, :])
         for turn in range(4):
             scatter.turn(turn)
+            if turn == 0:
+                gather_u.rest(3)
 
             @pl.when(inner)
             def _(turn=turn):

time: 353 us -> 352 us (level)
  no operation moved by 1% of the time
where the time goes in v4:
time: 352 us; the launch traced here: 346 us
  Pallas kernels  345 us (98%)
    pallas_call x1, Pallas kernels, run_main(): pl.pallas_call(functools.partial(main_kernel, (*args, *outs, *scratch)),...  338 us
    pallas_call x1, Pallas kernels, local(): pl.pallas_call(deliver_kernel, out_shape=(gain, gain, *(jax.ShapeDtypeStr...  7.84 us

profile of v4, /device:TPU:0, one launch (start us, length us, event | category | flops | bytes accessed | tf_op | source)
XLA Modules:
  0.0 346.4 jit_solution(10263153156483086863)
XLA Ops:
  0.6 337.6 %main.1 = (bf16[2,128,1536]{2,1,0:T(8,128)(2,1)}, bf16[2,128,1536]{2,1,0:T(8,128)(2,1)}, f32[3,192,768]{2,1,0:T(8,128)}, f32[192,768]{1,0:T(8,128)}, f32[192,307...) custom-call(s32[2]{0:T(128)} %refs_0_.1, ...), custom_call_target="tpu_custom_call" | custom-call | tf_op jit(solution)/shard_map/main/pallas_call | solution.py:1388
  338.3 7.8 %deliver.1 = (f32[1,96]{1,0:T(1,128)}, f32[1,96]{1,0:T(1,128)}, bf16[2,128,1536]{2,1,0:T(8,128)(2,1)}, bf16[2,128,1536]{2,1,0:T(8,128)(2,1)}, f32[3,192,768]{2,1...) custom-call(f32[8,768]{1,0:T(8,128)} %get-tuple-element.23.refs_0_, ...), custom_call_target="tpu_custom_call" | custom-call | tf_op jit(solution)/shard_map/deliver/pallas_call | solution.py:1433
